TPU v7x, 128 devices: a whole 4x4x4 slice. The times are simulated.
128 devices in a mesh: dp: 4 (over z_hi, core), ctx: 32 (over y, x, z_lo).
Axes of the slice: x: 4, y: 4, z: 4 (z_hi: 2, z_lo: 2; z = z_hi * 2 + z_lo), core: 2. Of those that a mesh axis runs over, the one named last changes fastest.
Arguments:
- q_gate: bfloat16 [4, 4096, 4096], P('dp', None, 'ctx'), may hold values from -6 to 6
- k_gate: bfloat16 [4, 4096, 4096], P('dp', None, 'ctx'), may hold values from -6 to 6
- values: bfloat16 [4, 4096, 4096], P('dp', None, 'ctx'), may hold values from -6 to 6
- grad_out: bfloat16 [4, 4096, 4096], P('dp', None, 'ctx'), may hold values from -6 to 6
- filt: float32 [4096, 4096], P(None, 'ctx'), may hold values from -6 to 6
Outputs:
- grad_query: bfloat16 [4, 4096, 4096], P('dp', None, 'ctx')
- grad_key: bfloat16 [4, 4096, 4096], P('dp', None, 'ctx')
- grad_value: bfloat16 [4, 4096, 4096], P('dp', None, 'ctx')
- filter_grad: float32 [4096, 4096], P('ctx', 'dp')
All inputs are finite; a program needn't handle non-finite values.
Results may differ from a plain program's by a relative error of at most 0.014.
Values may be sent and summed in bfloat16 or wider, within the bound.
No kernel may reach another device: no remote copies, remote signals or barrier semaphores. Data moves between devices by JAX's collectives and lax.ppermute only.
A program may use at most 128 MiB of HBM per device.

v0:
```python
import math

import jax
import jax.numpy as jnp
import numpy as np
from jax import lax
from jax.experimental import pallas as pl
from jax.experimental.pallas import tpu as pltpu
from jax.sharding import PartitionSpec as P

LENGTH = 4096
LANES = 128
BLOCKS = LENGTH // LANES
NSEQ = 4
GROUP = 32
UNROLL = 2
BF16 = jnp.bfloat16
F32 = jnp.float32


def split_table(table):
    high = table.astype(jnp.bfloat16).astype(np.float64)
    return high, table - high


def make_tables():
    rows = np.arange(BLOCKS) + 0.5
    block = np.arange(BLOCKS)
    lane = np.arange(LANES)
    phase = 2.0 * math.pi * rows[:, None] * block[None, :] / (2 * BLOCKS)
    first = np.concatenate([np.cos(phase), -np.sin(phase)], axis=0)
    first_high, first_low = split_table(first)
    first_both = np.concatenate([first_high, first_low], axis=1)
    last = np.concatenate([np.cos(phase.T), -np.sin(phase.T)], axis=1)
    last_high, last_low = split_table(last)
    last_both = np.concatenate([last_high, last_low], axis=1)
    angle = 2.0 * math.pi * rows[:, None] * lane[None, :] / (2 * LENGTH)
    twist = np.stack([np.cos(angle), -np.sin(angle)])
    scale = 1.0 / (LENGTH * math.sqrt(LENGTH))
    untwist = np.stack([np.cos(angle), np.sin(angle)]) * scale
    turn = 2.0 * math.pi * (lane[:, None] * lane[None, :] % LANES) / LANES
    cosine, sine = np.cos(turn), np.sin(turn)
    second = np.block([[cosine, -sine], [sine, cosine]])
    inverse = np.block([[cosine, sine], [-sine, cosine]])
    return (
        first_both.astype(jnp.bfloat16),
        twist.astype(np.float32),
        second.astype(jnp.bfloat16),
        inverse.astype(jnp.bfloat16),
        untwist.astype(np.float32),
        last_both.astype(jnp.bfloat16),
    )


def dot(left, right):
    return jnp.dot(left, right, preferred_element_type=F32)


def turn_by(real, imag, turn_real, turn_imag):
    return real * turn_real - imag * turn_imag, real * turn_imag + imag * turn_real


def pair(real, imag):
    return jnp.concatenate([real, imag], axis=1).astype(BF16)


def channel(signals, first, twist, second, inverse, untwist, last):
    count = len(signals)
    flat = jnp.concatenate(signals, axis=1).astype(BF16)
    part = dot(first, jnp.concatenate([flat, flat], axis=0))
    lines = []
    for s in range(count):
        cols = slice(s * LANES, (s + 1) * LANES)
        lines.append(pair(*turn_by(part[:BLOCKS, cols], part[BLOCKS:, cols], *twist)))
    spectrum = dot(jnp.concatenate(lines, axis=0), second)

    def spec(s):
        rows = slice(s * BLOCKS, (s + 1) * BLOCKS)
        return spectrum[rows, :LANES], spectrum[rows, LANES:]

    filt_real, filt_imag = spec(2 * NSEQ)
    convs, backs = [], []
    corr_real = corr_imag = None
    for n in range(NSEQ):
        in_real, in_imag = spec(n)
        grad_real, grad_imag = spec(NSEQ + n)
        convs.append(pair(*turn_by(in_real, in_imag, filt_real, filt_imag)))
        backs.append(pair(*turn_by(grad_real, grad_imag, filt_real, -filt_imag)))
        real, imag = turn_by(grad_real, grad_imag, in_real, -in_imag)
        corr_real = real if corr_real is None else corr_real + real
        corr_imag = imag if corr_imag is None else corr_imag + imag
    products = jnp.concatenate(convs + backs + [pair(corr_real, corr_imag)], axis=0)
    line = dot(products, inverse)
    columns = []
    for s in range(count):
        rows = slice(s * BLOCKS, (s + 1) * BLOCKS)
        real, imag = turn_by(line[rows, :LANES], line[rows, LANES:], *untwist)
        columns.append(jnp.concatenate([real, imag], axis=0))
    flat = jnp.concatenate(columns, axis=1).astype(BF16)
    return dot(last, jnp.concatenate([flat, flat], axis=0))


def convolve_kernel(
    x_ref, h_ref, first_ref, twist_ref, second_ref, inverse_ref, untwist_ref, last_ref,
    y_ref, corr_ref, x_wide, h_wide, y_wide, corr_wide,
):
    per_block = 2 * GROUP
    stride = NSEQ * per_block
    rows = 512

    def widen(step, carry):
        at = pl.ds(step * rows, rows)
        x_wide[at, :] = x_ref[at, :].astype(F32)
        return carry

    lax.fori_loop(0, x_ref.shape[0] // rows, widen, 0)
    h_wide[...] = h_ref[...].astype(F32)

    def body(step, carry):
        for inner in range(UNROLL):
            c = step * UNROLL + inner
            where = [pl.ds(n * per_block + part * GROUP + c, BLOCKS, stride=stride) for part in range(2) for n in range(NSEQ)]
            lag = pl.ds(c, BLOCKS, stride=GROUP)
            signals = [x_wide[at, :] for at in where] + [h_wide[lag, :]]
            out = channel(
                signals, first_ref[...], (twist_ref[0], twist_ref[1]), second_ref[...], inverse_ref[...],
                (untwist_ref[0], untwist_ref[1]), last_ref[...],
            )
            for s, at in enumerate(where):
                y_wide[at, :] = out[:, s * LANES:(s + 1) * LANES]
            corr_wide[lag, :] = out[:, 2 * NSEQ * LANES:]
        return carry

    lax.fori_loop(0, GROUP // UNROLL, body, 0)

    def narrow(step, carry):
        at = pl.ds(step * rows, rows)
        y_ref[at, :] = y_wide[at, :].astype(BF16)
        return carry

    lax.fori_loop(0, y_ref.shape[0] // rows, narrow, 0)
    corr_ref[...] = corr_wide[...].astype(BF16)


def convolve(x, h):
    tables = [jnp.asarray(table) for table in make_tables()]
    vmem = pl.BlockSpec(memory_space=pltpu.VMEM)
    return pl.pallas_call(
        convolve_kernel,
        out_shape=(jax.ShapeDtypeStruct(x.shape, BF16), jax.ShapeDtypeStruct(h.shape, BF16)),
        in_specs=[vmem] * 8,
        out_specs=(vmem, vmem),
        scratch_shapes=[
            pltpu.VMEM(x.shape, F32),
            pltpu.VMEM(h.shape, F32),
            pltpu.VMEM(x.shape, F32),
            pltpu.VMEM(h.shape, F32),
        ],
        compiler_params=pltpu.CompilerParams(vmem_limit_bytes=48 * 2**20),
        cost_estimate=pl.CostEstimate(flops=10**10, bytes_accessed=5 * 2**20, transcendentals=0),
        name="convolve",
    )(x, h, *tables)


def product(first, second):
    return (first.astype(F32) * second.astype(F32)).astype(BF16)


def gate_kernel(k_ref, v_ref, q_ref, g_ref, x_ref):
    x_ref[:, :GROUP, :] = product(k_ref[...], v_ref[...])
    x_ref[:, GROUP:, :] = product(g_ref[...], q_ref[...])


def gate(k, v, q, g):
    count = k.shape[0]
    step = 16
    part = pl.BlockSpec((step, GROUP, LANES), lambda i: (i, 0, 0))
    return pl.pallas_call(
        gate_kernel,
        grid=(count // step,),
        out_shape=jax.ShapeDtypeStruct((count, 2 * GROUP, LANES), BF16),
        in_specs=[part] * 4,
        out_specs=pl.BlockSpec((step, 2 * GROUP, LANES), lambda i: (i, 0, 0)),
        compiler_params=pltpu.CompilerParams(vmem_limit_bytes=32 * 2**20),
        name="gate",
    )(k, v, q, g)


def ungate_kernel(y_ref, k_ref, v_ref, g_ref, gq_ref, gk_ref, gv_ref):
    conv, back = y_ref[:, :GROUP, :], y_ref[:, GROUP:, :]
    gq_ref[...] = product(g_ref[...], conv)
    gk_ref[...] = product(back, v_ref[...])
    gv_ref[...] = product(back, k_ref[...])


def ungate(y, k, v, g):
    count = k.shape[0]
    step = 16
    part = pl.BlockSpec((step, GROUP, LANES), lambda i: (i, 0, 0))
    return pl.pallas_call(
        ungate_kernel,
        grid=(count // step,),
        out_shape=(jax.ShapeDtypeStruct(k.shape, BF16),) * 3,
        in_specs=[pl.BlockSpec((step, 2 * GROUP, LANES), lambda i: (i, 0, 0))] + [part] * 3,
        out_specs=(part,) * 3,
        compiler_params=pltpu.CompilerParams(vmem_limit_bytes=32 * 2**20),
        name="ungate",
    )(y, k, v, g)


def shards(q_gate, k_gate, values, grad_out, filt):
    every = ("ctx", "dp")
    shape = q_gate.shape
    count = shape[1] // GROUP
    q, k, v, g = (a.reshape(count, GROUP, LANES) for a in (q_gate, k_gate, values, grad_out))
    own = lax.axis_index("dp")
    lags = lax.dynamic_index_in_dim(filt.reshape(BLOCKS, NSEQ, GROUP, LANES), own, 1, keepdims=False)
    h = lax.all_to_all(lags.astype(BF16), "ctx", 0, 0, tiled=True)
    x = lax.all_to_all(gate(k, v, q, g), every, 0, 0, tiled=True)
    y, corr = convolve(x.reshape(count * 2 * GROUP, LANES), h.reshape(BLOCKS * GROUP, LANES))
    corr = lax.all_to_all(corr.reshape(BLOCKS, GROUP, LANES), "dp", 0, 0, tiled=True)
    y = lax.all_to_all(y.reshape(count, 2 * GROUP, LANES), every, 0, 0, tiled=True)
    grads = ungate(y, k, v, g)
    corr = corr.reshape(NSEQ, BLOCKS // NSEQ, GROUP, LANES).transpose(0, 2, 1, 3)
    filter_grad = corr.reshape(NSEQ * GROUP, LENGTH // NSEQ).astype(F32)
    return tuple(grad.reshape(shape) for grad in grads) + (filter_grad,)


def solution(mesh):
    part = P("dp", None, "ctx")
    return jax.shard_map(
        shards,
        mesh=mesh,
        in_specs=(part, part, part, part, P(None, "ctx")),
        out_specs=(part, part, part, P("ctx", "dp")),
        check_vma=False,
    )
```

profile of v0, /device:TPU:1, one launch (start us, length us, event | category | flops | bytes accessed | tf_op | source)
XLA Modules:
  0.0 140.2 jit_solution(6144688922683838450)
XLA Ops:
  0.6 0.0 copy-start
  0.6 1.6 %copy-done = f32[4096,128]{1,0:T(8,128)S(1)} copy-done((f32[4096,128]{1,0:T(8,128)S(1)}, f32[4096,128]{1,0:T(8,128)}, u32[]{:S(2)}) %copy-start) | copy-done | bytes 2097176
  2.2 0.7 fusion
  3.0 9.2 %all-to-all-start.1 = ((bf16[32,32,128]{2,1,0:T(8,128)(2,1)}), bf16[32,32,128]{2,1,0:T(8,128)(2,1)S(1)}, u32[]{:S(2)}, u32[]{:S(2)}) async-start(bf16[32,32,128]{2,1,0:T(8,128)(2,1)} %fusion), calls=%async_computation.1 | async-start | bytes 524288 | tf_op jit(solution)/shard_map/all_to_all | solution.py:218
  12.2 1.2 copy-done.2
  13.4 1.2 copy-done.4
  14.7 1.2 copy-done.6
  15.9 1.2 copy-done.9
  17.1 0.6 gate.1
  17.7 1.3 copy-done.1
  19.0 0.0 copy-start.14
  19.0 0.0 copy-start.15
  19.1 1.7 %all-to-all-done.1 = bf16[32,32,128]{2,1,0:T(8,128)(2,1)S(1)} async-done(((bf16[32,32,128]{2,1,0:T(8,128)(2,1)}), bf16[32,32,128]{2,1,0:T(8,128)(2,1)S(1)}, u32[]{:S(2)}, u32[]{:S(2)}) %all-to-all-start.1) | async-done | bytes 262176 | tf_op jit(solution)/shard_map/all_to_all | solution.py:218
  20.8 39.1 %all_to_all.20 = bf16[128,64,128]{2,1,0:T(8,128)(2,1)S(1)} all-to-all(bf16[128,64,128]{2,1,0:T(8,128)(2,1)} %copy-done.1), channel_id=1, replica_groups=mesh['dp'=4,'ctx'=32] {'ctx','dp'}, dimensions={0} | all-to-all | bytes 4194304 | tf_op jit(solution)/shard_map/all_to_all | solution.py:219
  59.9 24.8 %convolve.1 = (bf16[8192,128]{1,0:T(8,128)(2,1)S(1)}, bf16[1024,128]{1,0:T(8,128)(2,1)S(1)}) custom-call(bf16[8192,128]{1,0:T(8,128)(2,1)S(1)} %bitcast.34, bf16[1024,128]{1,0:T(8,128)(2,1)S(1)} %bitcast.36, bf16[64,64]{1,0:T(8,128)(2,1)S(1)} %copy-done.14, f32[2,32,128]{2,1,0:T(8,128)S(1)} %copy-done.12, bf16[256,256]{1,0:T(8,128)(2,1)S(1)} %copy-done.10, ...), custom_call_target="tpu_custom_call" | custom-call | flops 10000000000 | bytes 5242880 | tf_op jit(solution)/shard_map/convolve/pallas_call | solution.py:148
  84.7 1.3 copy-done.8
  86.0 10.1 %all_to_all.21 = bf16[32,32,128]{2,1,0:T(8,128)(2,1)S(1)} all-to-all(bf16[32,32,128]{2,1,0:T(8,128)(2,1)S(1)} %bitcast.37), channel_id=1, replica_groups=mesh['dp'=4,'ctx'=32] {'dp'}, dimensions={0} | all-to-all | bytes 524288 | tf_op jit(solution)/shard_map/all_to_all | solution.py:221
  96.2 5.7 %all-to-all-start.2 = ((bf16[128,64,128]{2,1,0:T(8,128)(2,1)}), bf16[128,64,128]{2,1,0:T(8,128)(2,1)}, u32[]{:S(2)}, u32[]{:S(2)}) async-start(bf16[128,64,128]{2,1,0:T(8,128)(2,1)} %bitcast.33), calls=%async_computation.2 | async-start | bytes 4194304 | tf_op jit(solution)/shard_map/all_to_all | solution.py:222
  101.8 0.1 copy.16
  101.9 0.9 copy.20
  102.8 29.0 %all-to-all-done.2.y_ref = bf16[128,64,128]{2,1,0:T(8,128)(2,1)} async-done(((bf16[128,64,128]{2,1,0:T(8,128)(2,1)}), bf16[128,64,128]{2,1,0:T(8,128)(2,1)}, u32[]{:S(2)}, u32[]{:S(2)}) %all-to-all-start.2) | async-done | bytes 2097184 | tf_op jit(solution)/shard_map/all_to_all | solution.py:222
  131.9 1.2 copy-done.5
  133.1 1.2 copy-done.7
  134.3 5.9 %ungate.1 = (bf16[128,32,128]{2,1,0:T(8,128)(2,1)}, bf16[128,32,128]{2,1,0:T(8,128)(2,1)}, bf16[128,32,128]{2,1,0:T(8,128)(2,1)}) custom-call(bf16[128,64,128]{2,1,0:T(8,128)(2,1)} %all-to-all-done.2.y_ref, bf16[128,32,128]{2,1,0:T(8,128)(2,1)S(1)} %bitcast.28, bf16[128,32,128]{2,1,0:T(8,128)(2,1)S(1)} %bitcast.30, bf16[128,32,128]{2,1,0:T(8,128)(2,1)S(1)} %bitcast.32), custom_call_target="tpu_custom_call" | custom-call | tf_op jit(solution)/shard_map/ungate/pallas_call | solution.py:200
  (20 shorter events, 0.0 us)
Async XLA Ops:
  0.6 1.6 %copy-start = (f32[4096,128]{1,0:T(8,128)S(1)}, f32[4096,128]{1,0:T(8,128)}, u32[]{:S(2)}) copy-start(f32[4096,128]{1,0:T(8,128)} %param.15) | copy-start | bytes 6291460
  3.0 17.8 %all-to-all-start.1 = ((bf16[32,32,128]{2,1,0:T(8,128)(2,1)}), bf16[32,32,128]{2,1,0:T(8,128)(2,1)S(1)}, u32[]{:S(2)}, u32[]{:S(2)}) async-start(bf16[32,32,128]{2,1,0:T(8,128)(2,1)} %fusion), calls=%async_computation.1 | async-start | bytes 524288 | tf_op jit(solution)/shard_map/all_to_all | solution.py:218
  12.2 1.2 copy-start.2
  13.4 1.2 copy-start.4
  14.7 1.2 copy-start.6
  15.9 1.2 copy-start.9
  17.7 1.3 copy-start.1
  19.0 40.9 %copy-start.10 = (bf16[256,256]{1,0:T(8,128)(2,1)S(1)}, bf16[256,256]{1,0:T(8,128)(2,1)}, u32[]{:S(2)}) copy-start(bf16[256,256]{1,0:T(8,128)(2,1)} %constant.26.clone.second_ref) | copy-start | bytes 393220
  19.0 40.9 %copy-start.11 = (bf16[256,256]{1,0:T(8,128)(2,1)S(1)}, bf16[256,256]{1,0:T(8,128)(2,1)}, u32[]{:S(2)}) copy-start(bf16[256,256]{1,0:T(8,128)(2,1)} %constant.27.clone.inverse_ref) | copy-start | bytes 393220
  19.0 40.9 %copy-start.12 = (f32[2,32,128]{2,1,0:T(8,128)S(1)}, f32[2,32,128]{2,1,0:T(8,128)}, u32[]{:S(2)}) copy-start(f32[2,32,128]{2,1,0:T(8,128)} %constant.25.clone.twist_ref) | copy-start | bytes 98308
  19.0 40.9 %copy-start.13 = (f32[2,32,128]{2,1,0:T(8,128)S(1)}, f32[2,32,128]{2,1,0:T(8,128)}, u32[]{:S(2)}) copy-start(f32[2,32,128]{2,1,0:T(8,128)} %constant.28.clone.untwist_ref) | copy-start | bytes 98308
  19.0 40.9 %copy-start.14 = (bf16[64,64]{1,0:T(8,128)(2,1)S(1)}, bf16[64,64]{1,0:T(8,128)(2,1)}, u32[]{:S(2)}) copy-start(bf16[64,64]{1,0:T(8,128)(2,1)} %constant.24.clone.first_ref) | copy-start | bytes 24580
  19.0 40.9 %copy-start.15 = (bf16[32,128]{1,0:T(8,128)(2,1)S(1)}, bf16[32,128]{1,0:T(8,128)(2,1)}, u32[]{:S(2)}) copy-start(bf16[32,128]{1,0:T(8,128)(2,1)} %constant.29.clone.last_ref) | copy-start | bytes 24580
  84.7 1.3 copy-start.8
  96.2 35.7 %copy-start.3 = (bf16[1,4096,128]{2,1,0:T(8,128)(2,1)S(1)}, bf16[1,4096,128]{2,1,0:T(8,128)(2,1)}, u32[]{:S(2)}) copy-start(bf16[1,4096,128]{2,1,0:T(8,128)(2,1)} %param.12) | copy-start | bytes 3145732
  96.2 35.7 %all-to-all-start.2 = ((bf16[128,64,128]{2,1,0:T(8,128)(2,1)}), bf16[128,64,128]{2,1,0:T(8,128)(2,1)}, u32[]{:S(2)}, u32[]{:S(2)}) async-start(bf16[128,64,128]{2,1,0:T(8,128)(2,1)} %bitcast.33), calls=%async_computation.2 | async-start | bytes 4194304 | tf_op jit(solution)/shard_map/all_to_all | solution.py:222
  131.9 1.2 copy-start.5
  133.1 1.2 copy-start.7
where the time goes:
time: 141 us; the launch traced here: 140 us
  blocking collectives  49.3 us (35%)
  Pallas kernels  31.2 us (22%)
  waiting for transfers between devices  30.7 us (22%)
  starting transfers between devices  14.9 us (11%)
  local copies, waits for them, and re-layouts  13.3 us (9%)
    all_to_all x1, blocking collectives, shards(): x = lax.all_to_all(gate(k, v, q, g), every, 0, 0, tiled=True)  39.1 us
    all_to_all x1, waiting for transfers between devices, shards(): lax.all_to_all(y.reshape(count, 2 * GROUP, LANES), every, 0, 0, tiled=True)  29 us
    pallas_call x1, Pallas kernels, convolve(): pl.pallas_call(convolve_kernel, out_shape=(jax.ShapeDtypeStruct(x.shape,...  24.8 us
    unnamed x33, local copies, waits for them, and re-layouts  12.5 us
    all_to_all x1, blocking collectives, shards(): lax.all_to_all(corr.reshape(BLOCKS, GROUP, LANES), 'dp', 0, 0, tiled=True)  10.1 us
    all_to_all x1, starting transfers between devices, shards(): h = lax.all_to_all(lags.astype(BF16), 'ctx', 0, 0, tiled=True)  9.22 us
    pallas_call x1, Pallas kernels, ungate(): pl.pallas_call(ungate_kernel, grid=(count // step,), out_shape=(jax.Shape...  5.88 us
    all_to_all x1, starting transfers between devices, shards(): lax.all_to_all(y.reshape(count, 2 * GROUP, LANES), every, 0, 0, tiled=True)  5.68 us
  transfers between devices with their start and end apart: 2, of which 2 were waited for; matrix products, arithmetic and copies ran while one was open for 1% of the time, Pallas kernels for 0%

commit v1 on v0

v1 whole, which is shorter than its diff:
```python
import math

import jax
import jax.numpy as jnp
import numpy as np
from jax import lax
from jax.experimental import pallas as pl
from jax.experimental.pallas import tpu as pltpu
from jax.sharding import PartitionSpec as P

LENGTH = 4096
LANES = 128
BLOCKS = LENGTH // LANES
NSEQ = 4
OCTET = 8
OCTETS = 4
GROUP = OCTET * OCTETS
SIGNALS = 2 * NSEQ + 1
ROWS = BLOCKS * OCTET
BF16 = jnp.bfloat16
F32 = jnp.float32


def make_tables():
    rows = np.arange(BLOCKS) + 0.5
    block = np.arange(BLOCKS)
    lane = np.arange(LANES)
    eye = np.eye(OCTET)
    phase = 2.0 * math.pi * rows[:, None] * block[None, :] / (2 * BLOCKS)
    first = np.kron(np.concatenate([np.cos(phase), -np.sin(phase)], axis=0), eye)
    last = np.kron(np.concatenate([np.cos(phase.T), -np.sin(phase.T)], axis=1), eye)
    angle = np.repeat(2.0 * math.pi * rows[:, None] * lane[None, :] / (2 * LENGTH), OCTET, axis=0)
    scale = 1.0 / (LENGTH * math.sqrt(LENGTH))
    twist = np.stack([np.cos(angle), -np.sin(angle)])
    untwist = np.stack([np.cos(angle), np.sin(angle)]) * scale
    turn = 2.0 * math.pi * (lane[:, None] * lane[None, :] % LANES) / LANES
    cosine, sine = np.cos(turn), np.sin(turn)
    second = np.block([[cosine, -sine], [sine, cosine]])
    inverse = np.block([[cosine, sine], [-sine, cosine]])
    return (
        first.astype(jnp.bfloat16),
        twist.astype(np.float32),
        second.astype(jnp.bfloat16),
        inverse.astype(jnp.bfloat16),
        untwist.astype(np.float32),
        last.astype(jnp.bfloat16),
    )


def dot(left, right):
    return jnp.dot(left, right, preferred_element_type=F32)


def turn_by(real, imag, turn_real, turn_imag):
    return real * turn_real - imag * turn_imag, real * turn_imag + imag * turn_real


def pair(real, imag):
    return jnp.concatenate([real, imag], axis=1).astype(BF16)


def octet(signals, first, twist, second, inverse, untwist, last):
    part = dot(first, jnp.concatenate(signals, axis=1))
    lines = []
    for s in range(SIGNALS):
        cols = slice(s * LANES, (s + 1) * LANES)
        lines.append(pair(*turn_by(part[:ROWS, cols], part[ROWS:, cols], *twist)))
    spectrum = dot(jnp.concatenate(lines, axis=0), second)

    def spec(s):
        rows = slice(s * ROWS, (s + 1) * ROWS)
        return spectrum[rows, :LANES], spectrum[rows, LANES:]

    filt_real, filt_imag = spec(2 * NSEQ)
    convs, backs = [], []
    corr_real = corr_imag = None
    for n in range(NSEQ):
        in_real, in_imag = spec(n)
        grad_real, grad_imag = spec(NSEQ + n)
        convs.append(pair(*turn_by(in_real, in_imag, filt_real, filt_imag)))
        backs.append(pair(*turn_by(grad_real, grad_imag, filt_real, -filt_imag)))
        real, imag = turn_by(grad_real, grad_imag, in_real, -in_imag)
        corr_real = real if corr_real is None else corr_real + real
        corr_imag = imag if corr_imag is None else corr_imag + imag
    line = dot(jnp.concatenate(convs + backs + [pair(corr_real, corr_imag)], axis=0), inverse)
    columns = []
    for s in range(SIGNALS):
        rows = slice(s * ROWS, (s + 1) * ROWS)
        real, imag = turn_by(line[rows, :LANES], line[rows, LANES:], *untwist)
        columns.append(jnp.concatenate([real, imag], axis=0))
    return dot(last, jnp.concatenate(columns, axis=1).astype(BF16))


def convolve_kernel(
    x_ref, h_ref, first_ref, twist_ref, second_ref, inverse_ref, untwist_ref, last_ref, y_ref, corr_ref,
):
    def rows_of(piece):
        return piece.astype(F32).reshape(ROWS, LANES).astype(BF16)

    signals = [rows_of(x_ref[:, n, part]) for part in range(2) for n in range(NSEQ)]
    signals.append(rows_of(h_ref[:, 0, 0]))
    out = octet(
        signals, first_ref[...], (twist_ref[0], twist_ref[1]), second_ref[...], inverse_ref[...],
        (untwist_ref[0], untwist_ref[1]), last_ref[...],
    )

    def blocks_of(s):
        return out[:, s * LANES:(s + 1) * LANES].reshape(BLOCKS, OCTET, LANES).astype(BF16)

    for n in range(NSEQ):
        for part in range(2):
            y_ref[:, n, part] = blocks_of(part * NSEQ + n)
    corr_ref[:, 0] = blocks_of(2 * NSEQ)


def convolve(x):
    tables = [jnp.asarray(table) for table in make_tables()]
    whole = [pl.BlockSpec(table.shape, lambda j, n=table.ndim: (0,) * n) for table in tables]
    both = pl.BlockSpec((BLOCKS, NSEQ, 2, OCTET, LANES), lambda j: (0, 0, j, 0, 0))
    return pl.pallas_call(
        convolve_kernel,
        grid=(OCTETS,),
        out_shape=(
            jax.ShapeDtypeStruct((BLOCKS, NSEQ, 2 * OCTETS, OCTET, LANES), BF16),
            jax.ShapeDtypeStruct((BLOCKS, OCTETS, OCTET, LANES), BF16),
        ),
        in_specs=[both, pl.BlockSpec((BLOCKS, 1, 1, OCTET, LANES), lambda j: (0, j, 2 * OCTETS, 0, 0))] + whole,
        out_specs=(both, pl.BlockSpec((BLOCKS, 1, OCTET, LANES), lambda j: (0, j, 0, 0))),
        compiler_params=pltpu.CompilerParams(vmem_limit_bytes=58 * 2**20),
        cost_estimate=pl.CostEstimate(flops=10**10, bytes_accessed=5 * 2**20, transcendentals=0),
        name="convolve",
    )(x, x, *tables)


def product(first, second):
    return first.astype(F32) * second.astype(F32)


def gate_kernel(own_ref, k_ref, v_ref, q_ref, g_ref, filt_ref, x_ref):
    mixed = product(k_ref[...], v_ref[...])
    grad_mix = product(g_ref[...], q_ref[...])
    for j in range(OCTETS):
        rows = slice(j * OCTET, (j + 1) * OCTET)
        x_ref[:, 2 * j] = mixed[:, rows].astype(BF16)
        x_ref[:, 2 * j + 1] = grad_mix[:, rows].astype(BF16)
    x_ref[:, 2 * OCTETS] = filt_ref[:, 0].astype(BF16)


def gate(own, k, v, q, g, filt):
    count = k.shape[0]
    step = 16
    part = pl.BlockSpec((step, GROUP, LANES), lambda i, own: (i, 0, 0))
    return pl.pallas_call(
        gate_kernel,
        out_shape=jax.ShapeDtypeStruct((count, SIGNALS, OCTET, LANES), BF16),
        grid_spec=pltpu.PrefetchScalarGridSpec(
            num_scalar_prefetch=1,
            grid=(count // step,),
            in_specs=[part] * 4 + [pl.BlockSpec((step, 1, OCTET, LANES), lambda i, own: (i, own[0], 0, 0))],
            out_specs=pl.BlockSpec((step, SIGNALS, OCTET, LANES), lambda i, own: (i, 0, 0, 0)),
        ),
        compiler_params=pltpu.CompilerParams(vmem_limit_bytes=58 * 2**20),
        name="gate",
    )(own, k, v, q, g, filt)


def ungate_kernel(y_ref, k_ref, v_ref, g_ref, gq_ref, gk_ref, gv_ref):
    conv = jnp.concatenate([y_ref[:, 2 * j].astype(F32) for j in range(OCTETS)], axis=1)
    back = jnp.concatenate([y_ref[:, 2 * j + 1].astype(F32) for j in range(OCTETS)], axis=1)
    gq_ref[...] = product(g_ref[...], conv).astype(BF16)
    gk_ref[...] = product(back, v_ref[...]).astype(BF16)
    gv_ref[...] = product(back, k_ref[...]).astype(BF16)


def ungate(y, k, v, g):
    count = k.shape[0]
    step = 16
    part = pl.BlockSpec((step, GROUP, LANES), lambda i: (i, 0, 0))
    return pl.pallas_call(
        ungate_kernel,
        grid=(count // step,),
        out_shape=(jax.ShapeDtypeStruct(k.shape, BF16),) * 3,
        in_specs=[pl.BlockSpec((step, 2 * OCTETS, OCTET, LANES), lambda i: (i, 0, 0, 0))] + [part] * 3,
        out_specs=(part,) * 3,
        compiler_params=pltpu.CompilerParams(vmem_limit_bytes=58 * 2**20),
        name="ungate",
    )(y, k, v, g)


def exchange_lags(corr, own):
    quarters = corr.reshape(NSEQ, BLOCKS // NSEQ, GROUP, LANES)
    got = [lax.dynamic_index_in_dim(quarters, own, 0, keepdims=False)]
    for shift in range(1, NSEQ):
        sent = lax.dynamic_index_in_dim(quarters, own ^ shift, 0, keepdims=False)
        got.append(lax.ppermute(sent, "dp", [(d, d ^ shift) for d in range(NSEQ)]))
    odd, high = own & 1, own & 2
    got = [jnp.where(odd == 1, got[s ^ 1], got[s]) for s in range(NSEQ)]
    got = [jnp.where(high == 2, got[s ^ 2], got[s]) for s in range(NSEQ)]
    merged = jnp.stack(got).transpose(0, 2, 1, 3)
    return merged.reshape(NSEQ * GROUP, LENGTH // NSEQ).astype(F32)


def shards(q_gate, k_gate, values, grad_out, filt):
    every = ("ctx", "dp")
    shape = q_gate.shape
    count = shape[1] // GROUP
    q, k, v, g = (a.reshape(count, GROUP, LANES) for a in (q_gate, k_gate, values, grad_out))
    own = lax.axis_index("dp")
    x = gate(own.reshape(1), k, v, q, g, filt.reshape(count, OCTETS, OCTET, LANES))
    x = lax.all_to_all(x, every, 0, 0, tiled=True)
    y, corr = convolve(x.reshape(BLOCKS, NSEQ, SIGNALS, OCTET, LANES))
    y = lax.all_to_all(y.reshape(count, 2 * OCTETS, OCTET, LANES), every, 0, 0, tiled=True)
    filter_grad = exchange_lags(corr, own)
    grads = ungate(y, k, v, g)
    return tuple(grad.reshape(shape) for grad in grads) + (filter_grad,)


def solution(mesh):
    part = P("dp", None, "ctx")
    return jax.shard_map(
        shards,
        mesh=mesh,
        in_specs=(part, part, part, part, P(None, "ctx")),
        out_specs=(part, part, part, P("ctx", "dp")),
        check_vma=False,
    )
```

time: 141 us -> 107 us (0.76)
  local copies, waits for them, and re-layouts: 13.3 us -> 2.56 us
  Pallas kernels: 31.2 us -> 23.9 us
  starting transfers between devices: 14.9 us -> 9.1 us
  waiting for transfers between devices: 30.7 us -> 25.7 us
  blocking collectives: 49.3 us -> 44.6 us
    all_to_all x2 -> x1, waiting for transfers between devices: 30.7 us -> 0.01 us  [shards(): lax.all_to_all(y.reshape(count, 2 * OCTETS, OCTET, LANES), every, 0, 0, t...]
    ppermute x0 -> x3, waiting for transfers between devices: none -> 25.7 us  [exchange_lags(): got.append(lax.ppermute(sent, 'dp', [(d, d ^ shift) for d in range(NSEQ)]))]
    unnamed x33 -> x5, local copies, waits for them, and re-layouts: 12.5 us -> 2.23 us
    all_to_all x2 -> x1, starting transfers between devices: 14.9 us -> 4.87 us  [shards(): lax.all_to_all(y.reshape(count, 2 * OCTETS, OCTET, LANES), every, 0, 0, t...]
    pallas_call x2, Pallas kernels: 25.3 us -> 17.4 us  [the longest x1 10.9 us: convolve(): pl.pallas_call(convolve_kernel, grid=(OCTETS,), out_shape=(jax.ShapeDtype...]
    all_to_all x2 -> x1, blocking collectives: 49.3 us -> 44.6 us  [shards(): x = lax.all_to_all(x, every, 0, 0, tiled=True)]
    ppermute x0 -> x3, starting transfers between devices: none -> 4.23 us  [exchange_lags(): got.append(lax.ppermute(sent, 'dp', [(d, d ^ shift) for d in range(NSEQ)]))]
  transfers between devices with their start and end apart: 2 -> 4, of which waited for: 2 -> 2; matrix products, arithmetic and copies ran while one was open for 1% -> 1% of each run, Pallas kernels for 0% -> 0%
where the time goes in v1:
time: 107 us
  blocking collectives  44.6 us (42%)
  waiting for transfers between devices  25.7 us (24%)
  Pallas kernels  23.9 us (22%)
  starting transfers between devices  9.1 us (9%)
  local copies, waits for them, and re-layouts  2.56 us (2%)
    all_to_all x1, blocking collectives, shards(): x = lax.all_to_all(x, every, 0, 0, tiled=True)  44.6 us
    ppermute x3, waiting for transfers between devices, exchange_lags(): got.append(lax.ppermute(sent, 'dp', [(d, d ^ shift) for d in range(NSEQ)]))  25.7 us
    pallas_call x1, Pallas kernels, convolve(): pl.pallas_call(convolve_kernel, grid=(OCTETS,), out_shape=(jax.ShapeDtype...  10.9 us
    pallas_call x1, Pallas kernels, ungate(): pl.pallas_call(ungate_kernel, grid=(count // step,), out_shape=(jax.Shape...  6.48 us
    pallas_call x1, Pallas kernels, gate(): pl.pallas_call(gate_kernel, out_shape=jax.ShapeDtypeStruct((count, SIGNAL...  6.45 us
    all_to_all x1, starting transfers between devices, shards(): lax.all_to_all(y.reshape(count, 2 * OCTETS, OCTET, LANES), every, 0, 0, t...  4.87 us
    ppermute x3, starting transfers between devices, exchange_lags(): got.append(lax.ppermute(sent, 'dp', [(d, d ^ shift) for d in range(NSEQ)]))  4.23 us
    unnamed x5, local copies, waits for them, and re-layouts  2.23 us
  transfers between devices with their start and end apart: 4, of which 2 were waited for; matrix products, arithmetic and copies ran while one was open for 1% of the time, Pallas kernels for 0%

profile of v1, /device:TPU:1, one launch (start us, length us, event | category | flops | bytes accessed | tf_op | source)
XLA Modules:
  0.0 106.6 jit_solution(500881347358361237)
XLA Ops:
  0.6 6.4 %gate.1 = bf16[128,9,8,128]{3,2,1,0:T(8,128)(2,1)} custom-call(s32[1]{0:T(128)} %bitcast.own_ref, bf16[128,32,128]{2,1,0:T(8,128)(2,1)} %bitcast.44, bf16[128,32,128]{2,1,0:T(8,128)(2,1)} %bitcast.46, bf16[128,32,128]{2,1,0:T(8,128)(2,1)} %bitcast.55, bf16[128,32,128]{2,1,0:T(8,128)(2,1)} %bitcast.48, f32[128,4,8,128]{3,2,1,0:T(8,128)} %bitcast.52), custom_call_target="tpu_custom_call" | custom-call | tf_op jit(solution)/shard_map/gate/pallas_call | solution.py:153
  7.1 44.6 %all_to_all.10 = bf16[128,9,8,128]{3,2,1,0:T(8,128)(2,1)} all-to-all(bf16[128,9,8,128]{3,2,1,0:T(8,128)(2,1)} %gate.1), channel_id=1, replica_groups=mesh['dp'=4,'ctx'=32] {'ctx','dp'}, dimensions={0} | all-to-all | bytes 4718592 | tf_op jit(solution)/shard_map/all_to_all | solution.py:210
  51.7 10.9 %convolve.1 = (bf16[32,4,8,8,128]{4,3,2,1,0:T(8,128)(2,1)}, bf16[32,4,8,128]{3,2,1,0:T(8,128)(2,1)}) custom-call(bf16[32,4,9,8,128]{4,3,2,1,0:T(8,128)(2,1)} %bitcast.50, bf16[32,4,9,8,128]{4,3,2,1,0:T(8,128)(2,1)} %bitcast.51, bf16[512,256]{1,0:T(8,128)(2,1)} %constant.36.clone.first_ref, f32[2,256,128]{2,1,0:T(8,128)} %constant.37.clone.twist_ref, ...), custom_call_target="tpu_custom_call" | custom-call | flops 10000000000 | bytes 5242880 | tf_op jit(solution)/shard_map/convolve/pallas_call | solution.py:120
  62.6 0.0 copy-start.1
  62.6 4.9 %all-to-all-start.1 = ((bf16[128,8,8,128]{3,2,1,0:T(8,128)(2,1)}), bf16[128,8,8,128]{3,2,1,0:T(8,128)(2,1)S(1)}, u32[]{:S(2)}, u32[]{:S(2)}) async-start(bf16[128,8,8,128]{3,2,1,0:T(8,128)(2,1)} %bitcast.53), calls=%async_computation.1 | async-start | bytes 4194304 | tf_op jit(solution)/shard_map/all_to_all | solution.py:212
  67.5 0.0 copy-done.1
  67.6 3.7 %collective-permute-start = (bf16[8,32,128]{2,1,0:T(8,128)(2,1)S(1)}, bf16[8,32,128]{2,1,0:T(8,128)(2,1)S(1)}, u32[]{:S(2)}, u32[]{:S(2)}) collective-permute-start(bf16[8,32,128]{2,1,0:T(8,128)(2,1)S(1)} %get-tuple-element.20), channel_id=1, source_target_pairs={{0,96},{32,64},{64,32},{96,0},{1,97},{33,65},{65,33},{97,1},{2,98}... | collective-permute-start | bytes 196616 | tf_op jit(solution)/shard_map/ppermute | solution.py:195
  71.3 0.4 collective-permute-start.1
  71.7 0.1 collective-permute-start.2
  71.8 20.0 %collective-permute-done = bf16[8,32,128]{2,1,0:T(8,128)(2,1)S(1)} collective-permute-done((bf16[8,32,128]{2,1,0:T(8,128)(2,1)S(1)}, bf16[8,32,128]{2,1,0:T(8,128)(2,1)S(1)}, u32[]{:S(2)}, u32[]{:S(2)}) %collective-permute-start) | collective-permute-done | bytes 65568 | tf_op jit(solution)/shard_map/ppermute | solution.py:195
  91.8 5.7 %collective-permute-done.1 = bf16[8,32,128]{2,1,0:T(8,128)(2,1)S(1)} collective-permute-done((bf16[8,32,128]{2,1,0:T(8,128)(2,1)S(1)}, bf16[8,32,128]{2,1,0:T(8,128)(2,1)S(1)}, u32[]{:S(2)}, u32[]{:S(2)}) %collective-permute-start.1) | collective-permute-done | bytes 65568 | tf_op jit(solution)/shard_map/ppermute | solution.py:195
  97.5 0.0 collective-permute-done.2
  97.6 0.3 copy.15
  97.9 0.9 copy.18
  98.8 0.0 all-to-all-done.1.y_ref
  98.8 0.0 copy-start
  98.8 1.3 %copy-done = bf16[128,8,8,128]{3,2,1,0:T(8,128)(2,1)} copy-done((bf16[128,8,8,128]{3,2,1,0:T(8,128)(2,1)}, bf16[128,8,8,128]{3,2,1,0:T(8,128)(2,1)S(1)}, u32[]{:S(2)}) %copy-start) | copy-done | bytes 2097176
  100.1 6.5 %ungate.1 = (bf16[128,32,128]{2,1,0:T(8,128)(2,1)}, bf16[128,32,128]{2,1,0:T(8,128)(2,1)}, bf16[128,32,128]{2,1,0:T(8,128)(2,1)}) custom-call(bf16[128,8,8,128]{3,2,1,0:T(8,128)(2,1)} %copy-done, bf16[128,32,128]{2,1,0:T(8,128)(2,1)} %bitcast.45, bf16[128,32,128]{2,1,0:T(8,128)(2,1)} %bitcast.47, bf16[128,32,128]{2,1,0:T(8,128)(2,1)} %bitcast.49), custom_call_target="tpu_custom_call" | custom-call | tf_op jit(solution)/shard_map/ungate/pallas_call | solution.py:179
  (3 shorter events, 0.1 us)
Async XLA Ops:
  62.6 4.9 %copy-start.1 = (bf16[32,4,8,128]{3,2,1,0:T(8,128)(2,1)S(1)}, bf16[32,4,8,128]{3,2,1,0:T(8,128)(2,1)}, u32[]{:S(2)}) copy-start(bf16[32,4,8,128]{3,2,1,0:T(8,128)(2,1)} %get-tuple-element.13) | copy-start | bytes 786436
  62.6 36.1 %all-to-all-start.1 = ((bf16[128,8,8,128]{3,2,1,0:T(8,128)(2,1)}), bf16[128,8,8,128]{3,2,1,0:T(8,128)(2,1)S(1)}, u32[]{:S(2)}, u32[]{:S(2)}) async-start(bf16[128,8,8,128]{3,2,1,0:T(8,128)(2,1)} %bitcast.53), calls=%async_computation.1 | async-start | bytes 4194304 | tf_op jit(solution)/shard_map/all_to_all | solution.py:212
  67.6 24.2 %collective-permute-start = (bf16[8,32,128]{2,1,0:T(8,128)(2,1)S(1)}, bf16[8,32,128]{2,1,0:T(8,128)(2,1)S(1)}, u32[]{:S(2)}, u32[]{:S(2)}) collective-permute-start(bf16[8,32,128]{2,1,0:T(8,128)(2,1)S(1)} %get-tuple-element.20), channel_id=1, source_target_pairs={{0,96},{32,64},{64,32},{96,0},{1,97},{33,65},{65,33},{97,1},{2,98}... | collective-permute-start | bytes 196616 | tf_op jit(solution)/shard_map/ppermute | solution.py:195
  71.3 26.2 %collective-permute-start.1 = (bf16[8,32,128]{2,1,0:T(8,128)(2,1)S(1)}, bf16[8,32,128]{2,1,0:T(8,128)(2,1)S(1)}, u32[]{:S(2)}, u32[]{:S(2)}) collective-permute-start(bf16[8,32,128]{2,1,0:T(8,128)(2,1)S(1)} %get-tuple-element.19), channel_id=1, source_target_pairs={{0,64},{32,96},{64,0},{96,32},{1,65},{33,97},{65,1},{97,33},{2,66}... | collective-permute-start | bytes 196616 | tf_op jit(solution)/shard_map/ppermute | solution.py:195
  71.7 25.8 %collective-permute-start.2 = (bf16[8,32,128]{2,1,0:T(8,128)(2,1)S(1)}, bf16[8,32,128]{2,1,0:T(8,128)(2,1)S(1)}, u32[]{:S(2)}, u32[]{:S(2)}) collective-permute-start(bf16[8,32,128]{2,1,0:T(8,128)(2,1)S(1)} %get-tuple-element.18), channel_id=1, source_target_pairs={{0,32},{32,0},{64,96},{96,64},{1,33},{33,1},{65,97},{97,65},{2,34}... | collective-permute-start | bytes 196616 | tf_op jit(solution)/shard_map/ppermute | solution.py:195
  98.8 1.3 %copy-start = (bf16[128,8,8,128]{3,2,1,0:T(8,128)(2,1)}, bf16[128,8,8,128]{3,2,1,0:T(8,128)(2,1)S(1)}, u32[]{:S(2)}) copy-start(bf16[128,8,8,128]{3,2,1,0:T(8,128)(2,1)S(1)} %all-to-all-done.1.y_ref) | copy-start | bytes 6291460

commit v2 on v1

--- a/solution.py
+++ b/solution.py
@@ -92,13 +92,15 @@
 
 
 def convolve_kernel(
-    x_ref, h_ref, first_ref, twist_ref, second_ref, inverse_ref, untwist_ref, last_ref, y_ref, corr_ref,
+    x_ref, first_ref, twist_ref, second_ref, inverse_ref, untwist_ref, last_ref, y_ref, corr_ref,
 ):
+    j = pl.program_id(0)
+
     def rows_of(piece):
         return piece.astype(F32).reshape(ROWS, LANES).astype(BF16)
 
-    signals = [rows_of(x_ref[:, n, part]) for part in range(2) for n in range(NSEQ)]
-    signals.append(rows_of(h_ref[:, 0, 0]))
+    signals = [rows_of(x_ref[:, n, 2 * j + part]) for part in range(2) for n in range(NSEQ)]
+    signals.append(rows_of(x_ref[:, j, 2 * OCTETS]))
     out = octet(
         signals, first_ref[...], (twist_ref[0], twist_ref[1]), second_ref[...], inverse_ref[...],
         (untwist_ref[0], untwist_ref[1]), last_ref[...],
@@ -113,10 +115,12 @@
     corr_ref[:, 0] = blocks_of(2 * NSEQ)
 
 
+def whole():
+    return pl.BlockSpec(memory_space=pltpu.VMEM)
+
+
 def convolve(x):
     tables = [jnp.asarray(table) for table in make_tables()]
-    whole = [pl.BlockSpec(table.shape, lambda j, n=table.ndim: (0,) * n) for table in tables]
-    both = pl.BlockSpec((BLOCKS, NSEQ, 2, OCTET, LANES), lambda j: (0, 0, j, 0, 0))
     return pl.pallas_call(
         convolve_kernel,
         grid=(OCTETS,),
@@ -124,67 +128,110 @@
             jax.ShapeDtypeStruct((BLOCKS, NSEQ, 2 * OCTETS, OCTET, LANES), BF16),
             jax.ShapeDtypeStruct((BLOCKS, OCTETS, OCTET, LANES), BF16),
         ),
-        in_specs=[both, pl.BlockSpec((BLOCKS, 1, 1, OCTET, LANES), lambda j: (0, j, 2 * OCTETS, 0, 0))] + whole,
-        out_specs=(both, pl.BlockSpec((BLOCKS, 1, OCTET, LANES), lambda j: (0, j, 0, 0))),
-        compiler_params=pltpu.CompilerParams(vmem_limit_bytes=58 * 2**20),
+        in_specs=[whole()] * (1 + len(tables)),
+        out_specs=(
+            pl.BlockSpec((BLOCKS, NSEQ, 2, OCTET, LANES), lambda j: (0, 0, j, 0, 0)),
+            pl.BlockSpec((BLOCKS, 1, OCTET, LANES), lambda j: (0, j, 0, 0)),
+        ),
+        compiler_params=pltpu.CompilerParams(vmem_limit_bytes=40 * 2**20),
         cost_estimate=pl.CostEstimate(flops=10**10, bytes_accessed=5 * 2**20, transcendentals=0),
         name="convolve",
-    )(x, x, *tables)
+    )(x, *tables)
 
 
 def product(first, second):
     return first.astype(F32) * second.astype(F32)
 
 
-def gate_kernel(own_ref, k_ref, v_ref, q_ref, g_ref, filt_ref, x_ref):
-    mixed = product(k_ref[...], v_ref[...])
-    grad_mix = product(g_ref[...], q_ref[...])
-    for j in range(OCTETS):
-        rows = slice(j * OCTET, (j + 1) * OCTET)
-        x_ref[:, 2 * j] = mixed[:, rows].astype(BF16)
-        x_ref[:, 2 * j + 1] = grad_mix[:, rows].astype(BF16)
-    x_ref[:, 2 * OCTETS] = filt_ref[:, 0].astype(BF16)
+PARTS = 4
+
+
+def gate_kernel(own_ref, k_ref, v_ref, q_ref, g_ref, filt_ref, x_ref, k_in, v_in, q_in, g_in, filt_in, x_out, in_sem, filt_sem, out_sem):
+    step = k_in.shape[0] // PARTS
+
+    def arrive(i):
+        at = pl.ds(i * step, step)
+        refs = ((k_ref, k_in), (v_ref, v_in), (q_ref, q_in), (g_ref, g_in))
+        copies = [pltpu.make_async_copy(a.at[at], b.at[at], in_sem.at[i, n]) for n, (a, b) in enumerate(refs)]
+        return copies + [pltpu.make_async_copy(filt_ref.at[at, own_ref[0]], filt_in.at[at], filt_sem.at[i])]
+
+    def leave(i):
+        at = pl.ds(i * step, step)
+        return pltpu.make_async_copy(x_out.at[at], x_ref.at[at], out_sem.at[i])
+
+    for i in range(PARTS):
+        for copy in arrive(i):
+            copy.start()
+    for i in range(PARTS):
+        for copy in arrive(i):
+            copy.wait()
+        at = pl.ds(i * step, step)
+        mixed = product(k_in[at], v_in[at])
+        grad_mix = product(g_in[at], q_in[at])
+        for j in range(OCTETS):
+            rows = slice(j * OCTET, (j + 1) * OCTET)
+            x_out[at, 2 * j] = mixed[:, rows].astype(BF16)
+            x_out[at, 2 * j + 1] = grad_mix[:, rows].astype(BF16)
+        x_out[at, 2 * OCTETS] = filt_in[at].astype(BF16)
+        leave(i).start()
+    for i in range(PARTS):
+        leave(i).wait()
 
 
 def gate(own, k, v, q, g, filt):
     count = k.shape[0]
-    step = 16
-    part = pl.BlockSpec((step, GROUP, LANES), lambda i, own: (i, 0, 0))
+    out = (count, SIGNALS, OCTET, LANES)
+    anywhere = pl.BlockSpec(memory_space=pl.ANY)
     return pl.pallas_call(
         gate_kernel,
-        out_shape=jax.ShapeDtypeStruct((count, SIGNALS, OCTET, LANES), BF16),
-        grid_spec=pltpu.PrefetchScalarGridSpec(
-            num_scalar_prefetch=1,
-            grid=(count // step,),
-            in_specs=[part] * 4 + [pl.BlockSpec((step, 1, OCTET, LANES), lambda i, own: (i, own[0], 0, 0))],
-            out_specs=pl.BlockSpec((step, SIGNALS, OCTET, LANES), lambda i, own: (i, 0, 0, 0)),
-        ),
+        out_shape=jax.ShapeDtypeStruct(out, BF16),
+        in_specs=[pl.BlockSpec(memory_space=pltpu.SMEM)] + [anywhere] * 5,
+        out_specs=anywhere,
+        scratch_shapes=[pltpu.VMEM(k.shape, BF16)] * 4
+        + [
+            pltpu.VMEM((count, OCTET, LANES), F32),
+            pltpu.VMEM(out, BF16),
+            pltpu.SemaphoreType.DMA((PARTS, 4)),
+            pltpu.SemaphoreType.DMA((PARTS,)),
+            pltpu.SemaphoreType.DMA((PARTS,)),
+        ],
         compiler_params=pltpu.CompilerParams(vmem_limit_bytes=58 * 2**20),
         name="gate",
     )(own, k, v, q, g, filt)
 
 
-def ungate_kernel(y_ref, k_ref, v_ref, g_ref, gq_ref, gk_ref, gv_ref):
-    conv = jnp.concatenate([y_ref[:, 2 * j].astype(F32) for j in range(OCTETS)], axis=1)
-    back = jnp.concatenate([y_ref[:, 2 * j + 1].astype(F32) for j in range(OCTETS)], axis=1)
-    gq_ref[...] = product(g_ref[...], conv).astype(BF16)
-    gk_ref[...] = product(back, v_ref[...]).astype(BF16)
-    gv_ref[...] = product(back, k_ref[...]).astype(BF16)
-
-
-def ungate(y, k, v, g):
+def ungate_kernel(own_ref, y_ref, k_ref, v_ref, g_ref, r0_ref, r1_ref, r2_ref, r3_ref, gq_ref, gk_ref, gv_ref, corr_ref):
+    i = pl.program_id(0)
+    step = gq_ref.shape[0]
+    at = pl.ds(i * step, step)
+    conv = jnp.concatenate([y_ref[at, 2 * j].astype(F32) for j in range(OCTETS)], axis=1)
+    back = jnp.concatenate([y_ref[at, 2 * j + 1].astype(F32) for j in range(OCTETS)], axis=1)
+    gq_ref[...] = product(g_ref[at], conv).astype(BF16)
+    gk_ref[...] = product(back, v_ref[at]).astype(BF16)
+    gv_ref[...] = product(back, k_ref[at]).astype(BF16)
+    source = i ^ own_ref[0]
+    for s, piece in enumerate((r0_ref, r1_ref, r2_ref, r3_ref)):
+
+        @pl.when(source == s)
+        def _(piece=piece):
+            for p in range(piece.shape[0]):
+                corr_ref[:, p * LANES:(p + 1) * LANES] = piece[p].astype(F32)
+
+
+def ungate(own, y, k, v, g, pieces):
     count = k.shape[0]
-    step = 16
+    step = count // NSEQ
     part = pl.BlockSpec((step, GROUP, LANES), lambda i: (i, 0, 0))
+    lags = LENGTH // NSEQ
     return pl.pallas_call(
         ungate_kernel,
-        grid=(count // step,),
-        out_shape=(jax.ShapeDtypeStruct(k.shape, BF16),) * 3,
-        in_specs=[pl.BlockSpec((step, 2 * OCTETS, OCTET, LANES), lambda i: (i, 0, 0, 0))] + [part] * 3,
-        out_specs=(part,) * 3,
-        compiler_params=pltpu.CompilerParams(vmem_limit_bytes=58 * 2**20),
+        grid=(NSEQ,),
+        out_shape=(jax.ShapeDtypeStruct(k.shape, BF16),) * 3 + (jax.ShapeDtypeStruct((NSEQ * GROUP, lags), F32),),
+        in_specs=[pl.BlockSpec(memory_space=pltpu.SMEM)] + [whole()] * 8,
+        out_specs=(part,) * 3 + (pl.BlockSpec((GROUP, lags), lambda i: (i, 0)),),
+        compiler_params=pltpu.CompilerParams(vmem_limit_bytes=24 * 2**20),
         name="ungate",
-    )(y, k, v, g)
+    )(own, y, k, v, g, *pieces)
 
 
 def exchange_lags(corr, own):
@@ -193,11 +240,7 @@
     for shift in range(1, NSEQ):
         sent = lax.dynamic_index_in_dim(quarters, own ^ shift, 0, keepdims=False)
         got.append(lax.ppermute(sent, "dp", [(d, d ^ shift) for d in range(NSEQ)]))
-    odd, high = own & 1, own & 2
-    got = [jnp.where(odd == 1, got[s ^ 1], got[s]) for s in range(NSEQ)]
-    got = [jnp.where(high == 2, got[s ^ 2], got[s]) for s in range(NSEQ)]
-    merged = jnp.stack(got).transpose(0, 2, 1, 3)
-    return merged.reshape(NSEQ * GROUP, LENGTH // NSEQ).astype(F32)
+    return got
 
 
 def shards(q_gate, k_gate, values, grad_out, filt):
@@ -206,12 +249,12 @@
     count = shape[1] // GROUP
     q, k, v, g = (a.reshape(count, GROUP, LANES) for a in (q_gate, k_gate, values, grad_out))
     own = lax.axis_index("dp")
-    x = gate(own.reshape(1), k, v, q, g, filt.reshape(count, OCTETS, OCTET, LANES))
+    slot = own.reshape(1)
+    x = gate(slot, k, v, q, g, filt.reshape(count, OCTETS, OCTET, LANES))
     x = lax.all_to_all(x, every, 0, 0, tiled=True)
     y, corr = convolve(x.reshape(BLOCKS, NSEQ, SIGNALS, OCTET, LANES))
     y = lax.all_to_all(y.reshape(count, 2 * OCTETS, OCTET, LANES), every, 0, 0, tiled=True)
-    filter_grad = exchange_lags(corr, own)
-    grads = ungate(y, k, v, g)
+    *grads, filter_grad = ungate(slot, y, k, v, g, exchange_lags(corr, own))
     return tuple(grad.reshape(shape) for grad in grads) + (filter_grad,)
 
 

time: 107 us -> 99.6 us (0.931)
  Pallas kernels: 23.9 us -> 15 us
  local copies, waits for them, and re-layouts: 2.56 us -> 3.86 us
    pallas_call x2, Pallas kernels: 12.9 us -> 6.18 us  [the longest x1 3.65 us: gate(): pl.pallas_call(gate_kernel, out_shape=jax.ShapeDtypeStruct(out, BF16), in...]
    pallas_call x1, Pallas kernels: 10.9 us -> 8.81 us  [convolve(): pl.pallas_call(convolve_kernel, grid=(OCTETS,), out_shape=(jax.ShapeDtype...]
    unnamed x5 -> x20, local copies, waits for them, and re-layouts: 2.23 us -> 3.83 us
  transfers between devices with their start and end apart: 4 -> 4, of which waited for: 2 -> 3; matrix products, arithmetic and copies ran while one was open for 1% -> 0% of each run, Pallas kernels for 0% -> 0%
where the time goes in v2:
time: 99.6 us; the launch traced here: 99.3 us
  blocking collectives  44.5 us (45%)
  waiting for transfers between devices  26.1 us (26%)
  Pallas kernels  15 us (15%)
  starting transfers between devices  9.09 us (9%)
  local copies, waits for them, and re-layouts  3.86 us (4%)
    all_to_all x1, blocking collectives, shards(): x = lax.all_to_all(x, every, 0, 0, tiled=True)  44.5 us
    ppermute x3, waiting for transfers between devices, exchange_lags(): got.append(lax.ppermute(sent, 'dp', [(d, d ^ shift) for d in range(NSEQ)]))  25.7 us
    pallas_call x1, Pallas kernels, convolve(): pl.pallas_call(convolve_kernel, grid=(OCTETS,), out_shape=(jax.ShapeDtype...  8.81 us
    all_to_all x1, starting transfers between devices, shards(): lax.all_to_all(y.reshape(count, 2 * OCTETS, OCTET, LANES), every, 0, 0, t...  4.85 us
    ppermute x3, starting transfers between devices, exchange_lags(): got.append(lax.ppermute(sent, 'dp', [(d, d ^ shift) for d in range(NSEQ)]))  4.23 us
    unnamed x20, local copies, waits for them, and re-layouts  3.83 us
    pallas_call x1, Pallas kernels, gate(): pl.pallas_call(gate_kernel, out_shape=jax.ShapeDtypeStruct(out, BF16), in...  3.65 us
    pallas_call x1, Pallas kernels, ungate(): pl.pallas_call(ungate_kernel, grid=(NSEQ,), out_shape=(jax.ShapeDtypeStru...  2.54 us
  transfers between devices with their start and end apart: 4, of which 3 were waited for; matrix products, arithmetic and copies ran while one was open for 0% of the time, Pallas kernels for 0%

profile of v2, /device:TPU:1, one launch (start us, length us, event | category | flops | bytes accessed | tf_op | source)
XLA Modules:
  0.0 99.3 jit_solution(4450019768236443571)
XLA Ops:
  0.6 3.6 %gate.1 = bf16[128,9,8,128]{3,2,1,0:T(8,128)(2,1)} custom-call(s32[1]{0:T(128)} %bitcast.own_ref, bf16[128,32,128]{2,1,0:T(8,128)(2,1)} %bitcast.20, bf16[128,32,128]{2,1,0:T(8,128)(2,1)} %bitcast.22, bf16[128,32,128]{2,1,0:T(8,128)(2,1)} %bitcast.30, bf16[128,32,128]{2,1,0:T(8,128)(2,1)} %bitcast.24, f32[128,4,8,128]{3,2,1,0:T(8,128)} %bitcast.29), custom_call_target="tpu_custom_call" | custom-call | tf_op jit(solution)/shard_map/gate/pallas_call | solution.py:185
  4.3 0.0 copy-start.4
  4.3 0.0 copy-start.5
  4.3 0.0 copy-start.6
  4.3 0.0 copy-start.7
  4.3 0.0 copy-start.8
  4.4 0.0 copy-start.9
  4.4 44.5 %all_to_all.10 = bf16[128,9,8,128]{3,2,1,0:T(8,128)(2,1)S(1)} all-to-all(bf16[128,9,8,128]{3,2,1,0:T(8,128)(2,1)} %gate.1), channel_id=1, replica_groups=mesh['dp'=4,'ctx'=32] {'ctx','dp'}, dimensions={0} | all-to-all | bytes 4718592 | tf_op jit(solution)/shard_map/all_to_all | solution.py:254
  48.9 0.0 copy-done.7
  48.9 0.0 copy-done.8
  48.9 0.0 copy-done.9
  48.9 8.8 %convolve.1 = (bf16[32,4,8,8,128]{4,3,2,1,0:T(8,128)(2,1)S(1)}, bf16[32,4,8,128]{3,2,1,0:T(8,128)(2,1)S(1)}) custom-call(bf16[32,4,9,8,128]{4,3,2,1,0:T(8,128)(2,1)S(1)} %bitcast.26, bf16[512,256]{1,0:T(8,128)(2,1)S(1)} %copy-done.7, f32[2,256,128]{2,1,0:T(8,128)S(1)} %copy-done.6, bf16[256,256]{1,0:T(8,128)(2,1)S(1)} %copy-done.9, ...), custom_call_target="tpu_custom_call" | custom-call | flops 10000000000 | bytes 5242880 | tf_op jit(solution)/shard_map/convolve/pallas_call | solution.py:124
  57.8 1.3 %copy-done.3 = bf16[32,4,8,8,128]{4,3,2,1,0:T(8,128)(2,1)} copy-done((bf16[32,4,8,8,128]{4,3,2,1,0:T(8,128)(2,1)}, bf16[32,4,8,8,128]{4,3,2,1,0:T(8,128)(2,1)S(1)}, u32[]{:S(2)}) %copy-start.3) | copy-done | bytes 2097176
  59.1 4.9 %all-to-all-start.1 = ((bf16[128,8,8,128]{3,2,1,0:T(8,128)(2,1)}), bf16[128,8,8,128]{3,2,1,0:T(8,128)(2,1)S(1)}, u32[]{:S(2)}, u32[]{:S(2)}) async-start(bf16[128,8,8,128]{3,2,1,0:T(8,128)(2,1)} %bitcast.27), calls=%async_computation.1 | async-start | bytes 4194304 | tf_op jit(solution)/shard_map/all_to_all | solution.py:256
  64.0 3.7 %collective-permute-start.2 = (bf16[8,32,128]{2,1,0:T(8,128)(2,1)S(1)}, bf16[8,32,128]{2,1,0:T(8,128)(2,1)S(1)}, u32[]{:S(2)}, u32[]{:S(2)}) collective-permute-start(bf16[8,32,128]{2,1,0:T(8,128)(2,1)S(1)} %get-tuple-element.16), channel_id=1, source_target_pairs={{0,96},{32,64},{64,32},{96,0},{1,97},{33,65},{65,33},{97,1},{2,98}... | collective-permute-start | bytes 196616 | tf_op jit(solution)/shard_map/ppermute | solution.py:242
  67.7 0.4 collective-permute-start.1
  68.1 0.1 collective-permute-start
  68.2 20.0 %collective-permute-done.2.r3_ref = bf16[8,32,128]{2,1,0:T(8,128)(2,1)S(1)} collective-permute-done((bf16[8,32,128]{2,1,0:T(8,128)(2,1)S(1)}, bf16[8,32,128]{2,1,0:T(8,128)(2,1)S(1)}, u32[]{:S(2)}, u32[]{:S(2)}) %collective-permute-start.2) | collective-permute-done | bytes 65568 | tf_op jit(solution)/shard_map/ppermute | solution.py:242
  88.3 5.7 %collective-permute-done.1.r2_ref = bf16[8,32,128]{2,1,0:T(8,128)(2,1)S(1)} collective-permute-done((bf16[8,32,128]{2,1,0:T(8,128)(2,1)S(1)}, bf16[8,32,128]{2,1,0:T(8,128)(2,1)S(1)}, u32[]{:S(2)}, u32[]{:S(2)}) %collective-permute-start.1) | collective-permute-done | bytes 65568 | tf_op jit(solution)/shard_map/ppermute | solution.py:242
  93.9 0.0 collective-permute-done.r1_ref
  93.9 0.4 all-to-all-done.1.y_ref
  94.3 1.2 %copy-done.1 = bf16[1,4096,128]{2,1,0:T(8,128)(2,1)S(1)} copy-done((bf16[1,4096,128]{2,1,0:T(8,128)(2,1)S(1)}, bf16[1,4096,128]{2,1,0:T(8,128)(2,1)}, u32[]{:S(2)}) %copy-start.1) | copy-done | bytes 1048600
  95.6 1.2 %copy-done.2 = bf16[1,4096,128]{2,1,0:T(8,128)(2,1)S(1)} copy-done((bf16[1,4096,128]{2,1,0:T(8,128)(2,1)S(1)}, bf16[1,4096,128]{2,1,0:T(8,128)(2,1)}, u32[]{:S(2)}) %copy-start.2) | copy-done | bytes 1048600
  96.8 2.5 %ungate.1 = (bf16[128,32,128]{2,1,0:T(8,128)(2,1)}, bf16[128,32,128]{2,1,0:T(8,128)(2,1)}, bf16[128,32,128]{2,1,0:T(8,128)(2,1)}, f32[128,1024]{1,0:T(8,128)}) custom-call(s32[1]{0:T(128)} %bitcast.own_ref, bf16[128,8,8,128]{3,2,1,0:T(8,128)(2,1)S(1)} %all-to-all-done.1.y_ref, bf16[128,32,128]{2,1,0:T(8,128)(2,1)S(1)} %bitcast.21, ...), custom_call_target="tpu_custom_call" | custom-call | tf_op jit(solution)/shard_map/ungate/pallas_call | solution.py:226
  (9 shorter events, 0.0 us)
Async XLA Ops:
  4.3 44.6 %copy-start.4 = (bf16[256,512]{1,0:T(8,128)(2,1)S(1)}, bf16[256,512]{1,0:T(8,128)(2,1)}, u32[]{:S(2)}) copy-start(bf16[256,512]{1,0:T(8,128)(2,1)} %constant.41.clone.last_ref) | copy-start | bytes 786436
  4.3 44.6 %copy-start.5 = (f32[2,256,128]{2,1,0:T(8,128)S(1)}, f32[2,256,128]{2,1,0:T(8,128)}, u32[]{:S(2)}) copy-start(f32[2,256,128]{2,1,0:T(8,128)} %constant.40.clone.untwist_ref) | copy-start | bytes 786436
  4.3 44.6 %copy-start.6 = (f32[2,256,128]{2,1,0:T(8,128)S(1)}, f32[2,256,128]{2,1,0:T(8,128)}, u32[]{:S(2)}) copy-start(f32[2,256,128]{2,1,0:T(8,128)} %constant.37.clone.twist_ref) | copy-start | bytes 786436
  4.3 44.6 %copy-start.7 = (bf16[512,256]{1,0:T(8,128)(2,1)S(1)}, bf16[512,256]{1,0:T(8,128)(2,1)}, u32[]{:S(2)}) copy-start(bf16[512,256]{1,0:T(8,128)(2,1)} %constant.36.clone.first_ref) | copy-start | bytes 786436
  4.3 44.6 %copy-start.8 = (bf16[256,256]{1,0:T(8,128)(2,1)S(1)}, bf16[256,256]{1,0:T(8,128)(2,1)}, u32[]{:S(2)}) copy-start(bf16[256,256]{1,0:T(8,128)(2,1)} %constant.39.clone.inverse_ref) | copy-start | bytes 393220
  4.4 44.6 %copy-start.9 = (bf16[256,256]{1,0:T(8,128)(2,1)S(1)}, bf16[256,256]{1,0:T(8,128)(2,1)}, u32[]{:S(2)}) copy-start(bf16[256,256]{1,0:T(8,128)(2,1)} %constant.38.clone.second_ref) | copy-start | bytes 393220
  57.7 1.3 %copy-start.3 = (bf16[32,4,8,8,128]{4,3,2,1,0:T(8,128)(2,1)}, bf16[32,4,8,8,128]{4,3,2,1,0:T(8,128)(2,1)S(1)}, u32[]{:S(2)}) copy-start(bf16[32,4,8,8,128]{4,3,2,1,0:T(8,128)(2,1)S(1)} %get-tuple-element.10) | copy-start | bytes 6291460
  59.1 35.2 %copy-start = (bf16[1,4096,128]{2,1,0:T(8,128)(2,1)S(1)}, bf16[1,4096,128]{2,1,0:T(8,128)(2,1)}, u32[]{:S(2)}) copy-start(bf16[1,4096,128]{2,1,0:T(8,128)(2,1)} %param.12) | copy-start | bytes 3145732
  59.1 35.2 %all-to-all-start.1 = ((bf16[128,8,8,128]{3,2,1,0:T(8,128)(2,1)}), bf16[128,8,8,128]{3,2,1,0:T(8,128)(2,1)S(1)}, u32[]{:S(2)}, u32[]{:S(2)}) async-start(bf16[128,8,8,128]{3,2,1,0:T(8,128)(2,1)} %bitcast.27), calls=%async_computation.1 | async-start | bytes 4194304 | tf_op jit(solution)/shard_map/all_to_all | solution.py:256
  64.0 24.3 %collective-permute-start.2 = (bf16[8,32,128]{2,1,0:T(8,128)(2,1)S(1)}, bf16[8,32,128]{2,1,0:T(8,128)(2,1)S(1)}, u32[]{:S(2)}, u32[]{:S(2)}) collective-permute-start(bf16[8,32,128]{2,1,0:T(8,128)(2,1)S(1)} %get-tuple-element.16), channel_id=1, source_target_pairs={{0,96},{32,64},{64,32},{96,0},{1,97},{33,65},{65,33},{97,1},{2,98}... | collective-permute-start | bytes 196616 | tf_op jit(solution)/shard_map/ppermute | solution.py:242
  67.7 26.2 %collective-permute-start.1 = (bf16[8,32,128]{2,1,0:T(8,128)(2,1)S(1)}, bf16[8,32,128]{2,1,0:T(8,128)(2,1)S(1)}, u32[]{:S(2)}, u32[]{:S(2)}) collective-permute-start(bf16[8,32,128]{2,1,0:T(8,128)(2,1)S(1)} %get-tuple-element.17), channel_id=1, source_target_pairs={{0,64},{32,96},{64,0},{96,32},{1,65},{33,97},{65,1},{97,33},{2,66}... | collective-permute-start | bytes 196616 | tf_op jit(solution)/shard_map/ppermute | solution.py:242
  68.1 25.8 %collective-permute-start = (bf16[8,32,128]{2,1,0:T(8,128)(2,1)S(1)}, bf16[8,32,128]{2,1,0:T(8,128)(2,1)S(1)}, u32[]{:S(2)}, u32[]{:S(2)}) collective-permute-start(bf16[8,32,128]{2,1,0:T(8,128)(2,1)S(1)} %get-tuple-element.18), channel_id=1, source_target_pairs={{0,32},{32,0},{64,96},{96,64},{1,33},{33,1},{65,97},{97,65},{2,34}... | collective-permute-start | bytes 196616 | tf_op jit(solution)/shard_map/ppermute | solution.py:242
  94.3 1.2 %copy-start.1 = (bf16[1,4096,128]{2,1,0:T(8,128)(2,1)S(1)}, bf16[1,4096,128]{2,1,0:T(8,128)(2,1)}, u32[]{:S(2)}) copy-start(bf16[1,4096,128]{2,1,0:T(8,128)(2,1)} %param.13) | copy-start | bytes 3145732
  95.6 1.2 %copy-start.2 = (bf16[1,4096,128]{2,1,0:T(8,128)(2,1)S(1)}, bf16[1,4096,128]{2,1,0:T(8,128)(2,1)}, u32[]{:S(2)}) copy-start(bf16[1,4096,128]{2,1,0:T(8,128)(2,1)} %param.14) | copy-start | bytes 3145732

commit v3 on v2

v3 whole, which is shorter than its diff:
```python
import math

import jax
import jax.numpy as jnp
import numpy as np
from jax import lax
from jax.experimental import pallas as pl
from jax.experimental.pallas import tpu as pltpu
from jax.sharding import Mesh, PartitionSpec as P

LENGTH = 4096
LANES = 128
BLOCKS = LENGTH // LANES
NSEQ = 4
OCTET = 8
OCTETS = 4
GROUP = OCTET * OCTETS
SIGNALS = 2 * NSEQ + 1
ROWS = BLOCKS * OCTET
BF16 = jnp.bfloat16
F32 = jnp.float32

SPLIT = {"zh": 2, "k": 2, "y": 4, "x": 4, "zl": 2}
DP, CTX = ("zh", "k"), ("y", "x", "zl")
ORDER = ("zl", "zh", "x", "k", "y")
LEAD = tuple(SPLIT[axis] for axis in ORDER)


def make_tables():
    rows = np.arange(BLOCKS) + 0.5
    block = np.array([y * 8 + x * 2 + zl for zl in range(2) for x in range(4) for y in range(4)])
    lane = np.arange(LANES)
    eye = np.eye(OCTET)
    phase = 2.0 * math.pi * rows[:, None] * block[None, :] / (2 * BLOCKS)
    first = np.stack([np.cos(phase), -np.sin(phase)], axis=1).reshape(2 * BLOCKS, BLOCKS)
    angle = np.repeat(2.0 * math.pi * rows[:, None] * lane[None, :] / (2 * LENGTH), OCTET, axis=0)
    scale = 1.0 / (LENGTH * math.sqrt(LENGTH))
    twist = np.stack([np.cos(angle), -np.sin(angle)])
    untwist = np.stack([np.cos(angle), np.sin(angle)]) * scale
    turn = 2.0 * math.pi * (lane[:, None] * lane[None, :] % LANES) / LANES
    cosine, sine = np.cos(turn), np.sin(turn)
    second = np.block([[cosine, -sine], [sine, cosine]])
    inverse = np.block([[cosine, sine], [-sine, cosine]])
    return (
        np.kron(first, eye).astype(jnp.bfloat16),
        twist.astype(np.float32),
        second.astype(jnp.bfloat16),
        inverse.astype(jnp.bfloat16),
        untwist.astype(np.float32),
        np.kron(first.T, eye).astype(jnp.bfloat16),
    )


def dot(left, right):
    return jnp.dot(left, right, preferred_element_type=F32)


def turn_by(real, imag, turn_real, turn_imag):
    return real * turn_real - imag * turn_imag, real * turn_imag + imag * turn_real


def pair(real, imag):
    return jnp.concatenate([real, imag], axis=1).astype(BF16)


def octet(signals, first, twist, second, inverse, untwist, last):
    spectra = []
    for s in range(0, SIGNALS, 2):
        both = signals[s:s + 2]
        width = len(both) * LANES
        part = dot(first, jnp.concatenate(both, axis=1)).reshape(BLOCKS, 2, OCTET, width)
        real, imag = part[:, 0].reshape(ROWS, width), part[:, 1].reshape(ROWS, width)
        for at in range(0, width, LANES):
            line = pair(*turn_by(real[:, at:at + LANES], imag[:, at:at + LANES], *twist))
            spectrum = dot(line, second)
            spectra.append((spectrum[:, :LANES], spectrum[:, LANES:]))
    filt_real, filt_imag = spectra[2 * NSEQ]
    convs, backs = [], []
    corr_real = corr_imag = None
    for n in range(NSEQ):
        in_real, in_imag = spectra[n]
        grad_real, grad_imag = spectra[NSEQ + n]
        convs.append(pair(*turn_by(in_real, in_imag, filt_real, filt_imag)))
        backs.append(pair(grad_real * filt_real + grad_imag * filt_imag, grad_imag * filt_real - grad_real * filt_imag))
        real = grad_real * in_real + grad_imag * in_imag
        imag = grad_imag * in_real - grad_real * in_imag
        corr_real = real if corr_real is None else corr_real + real
        corr_imag = imag if corr_imag is None else corr_imag + imag
    columns = []
    for product_spectrum in convs + backs + [pair(corr_real, corr_imag)]:
        line = dot(product_spectrum, inverse)
        real, imag = turn_by(line[:, :LANES], line[:, LANES:], *untwist)
        mixed = jnp.stack([real.reshape(BLOCKS, OCTET, LANES), imag.reshape(BLOCKS, OCTET, LANES)], axis=1)
        columns.append(mixed.reshape(2 * ROWS, LANES).astype(BF16))
    results = []
    for s in range(0, SIGNALS, 2):
        out = dot(last, jnp.concatenate(columns[s:s + 2], axis=1))
        results += [out[:, at:at + LANES] for at in range(0, out.shape[1], LANES)]
    return results


def convolve_kernel(
    x_ref, first_ref, twist_ref, second_ref, inverse_ref, untwist_ref, last_ref, y_ref, corr_ref,
):
    step = pl.program_id(0)

    def rows_of(piece):
        return piece.astype(F32).reshape(ROWS, LANES).astype(BF16)

    for o in range(SPLIT["k"]):
        j = step * SPLIT["k"] + o
        signals = [rows_of(x_ref[:, n // 2, :, n % 2, :, 2 * j + part]) for part in range(2) for n in range(NSEQ)]
        signals.append(rows_of(x_ref[:, step, :, o, :, 2 * OCTETS]))
        out = octet(
            signals, first_ref[...], (twist_ref[0], twist_ref[1]), second_ref[...], inverse_ref[...],
            (untwist_ref[0], untwist_ref[1]), last_ref[...],
        )
        out = [piece.reshape(2, 4, 4, OCTET, LANES).astype(BF16) for piece in out]
        for n in range(NSEQ):
            for part in range(2):
                y_ref[:, n // 2, :, n % 2, :, 2 * o + part] = out[part * NSEQ + n]
        for zl in range(2):
            for x in range(4):
                corr_ref[:, x, zl, o] = out[2 * NSEQ][zl, x]


def whole():
    return pl.BlockSpec(memory_space=pltpu.VMEM)


def convolve(x):
    tables = [jnp.asarray(table) for table in make_tables()]
    per = SPLIT["k"]
    return pl.pallas_call(
        convolve_kernel,
        grid=(OCTETS // per,),
        out_shape=(
            pltpu.HBM(LEAD + (2 * OCTETS, OCTET, LANES), BF16),
            jax.ShapeDtypeStruct((4, 4, 2, OCTETS, OCTET, LANES), BF16),
        ),
        in_specs=[whole()] * (1 + len(tables)),
        out_specs=(
            pl.BlockSpec(LEAD + (2 * per, OCTET, LANES), lambda j: (0, 0, 0, 0, 0, j, 0, 0)),
            pl.BlockSpec((4, 4, 2, per, OCTET, LANES), lambda j: (0, 0, 0, j, 0, 0)),
        ),
        compiler_params=pltpu.CompilerParams(vmem_limit_bytes=44 * 2**20),
        cost_estimate=pl.CostEstimate(flops=10**10, bytes_accessed=5 * 2**20, transcendentals=0),
        name="convolve",
    )(x, *tables)


def product(first, second):
    return first.astype(F32) * second.astype(F32)


def gate_kernel(
    own_ref, k_ref, v_ref, q_ref, g_ref, filt_ref, x_out, k_in, v_in, g_in, q_in, filt_in, in_sem, filt_sem,
):
    parts = SPLIT["y"]
    step = k_in.shape[0] // parts

    def arrive(y):
        at = pl.ds(y * step, step)
        refs = ((k_ref, k_in), (v_ref, v_in), (q_ref, q_in), (g_ref, g_in))
        copies = [pltpu.make_async_copy(a.at[at], b.at[at], in_sem.at[y, n]) for n, (a, b) in enumerate(refs)]
        return copies + [pltpu.make_async_copy(filt_ref.at[at, own_ref[0]], filt_in.at[at], filt_sem.at[y])]

    for y in range(parts):
        for copy in arrive(y):
            copy.start()
    for y in range(parts):
        for copy in arrive(y):
            copy.wait()
        at = pl.ds(y * step, step)
        mixed = product(k_in[at], v_in[at]).reshape(4, 2, 2, 2, GROUP, LANES)
        grad_mix = product(g_in[at], q_in[at]).reshape(4, 2, 2, 2, GROUP, LANES)
        lags = filt_in[at].reshape(4, 2, 2, 2, OCTET, LANES)
        for zl in range(2):
            for zh in range(2):
                for j in range(OCTETS):
                    rows = slice(j * OCTET, (j + 1) * OCTET)
                    x_out[zl, zh, :, :, y, 2 * j] = mixed[:, zl, zh, :, rows].astype(BF16)
                    x_out[zl, zh, :, :, y, 2 * j + 1] = grad_mix[:, zl, zh, :, rows].astype(BF16)
                x_out[zl, zh, :, :, y, 2 * OCTETS] = lags[:, zl, zh].astype(BF16)


def gate(own, k, v, q, g, filt):
    count = k.shape[0]
    parts = SPLIT["y"]
    far = pl.BlockSpec(memory_space=pltpu.HBM)
    kept = jax.ShapeDtypeStruct(k.shape, BF16)
    return pl.pallas_call(
        gate_kernel,
        out_shape=(jax.ShapeDtypeStruct(LEAD + (SIGNALS, OCTET, LANES), BF16), kept, kept, kept),
        in_specs=[pl.BlockSpec(memory_space=pltpu.SMEM)] + [far] * 5,
        out_specs=(whole(),) * 4,
        scratch_shapes=[
            pltpu.VMEM(k.shape, BF16),
            pltpu.VMEM((count, OCTET, LANES), F32),
            pltpu.SemaphoreType.DMA((parts, 4)),
            pltpu.SemaphoreType.DMA((parts,)),
        ],
        compiler_params=pltpu.CompilerParams(vmem_limit_bytes=24 * 2**20),
        name="gate",
    )(own, k, v, q, g, filt)


def ungate_kernel(own_ref, y_ref, k_ref, v_ref, g_ref, r0_ref, r1_ref, r2_ref, r3_ref, gq_ref, gk_ref, gv_ref, corr_ref):
    i = pl.program_id(0)
    step = gq_ref.shape[0]
    for x in range(4):
        for zl in range(2):
            for zh in range(2):
                row = x * 8 + zl * 4 + zh * 2
                here, there = pl.ds(row, 2), pl.ds(i * step + row, 2)
                conv, back = (
                    jnp.concatenate([y_ref[zl, zh, x, :, i, 2 * j + part].astype(F32) for j in range(OCTETS)], axis=1)
                    for part in range(2)
                )
                gq_ref[here] = product(g_ref[there], conv).astype(BF16)
                gk_ref[here] = product(back, v_ref[there]).astype(BF16)
                gv_ref[here] = product(back, k_ref[there]).astype(BF16)
    source = i ^ own_ref[0]
    for s, piece in enumerate((r0_ref, r1_ref, r2_ref, r3_ref)):

        @pl.when(source == s)
        def _(piece=piece):
            for p in range(piece.shape[0]):
                corr_ref[:, p * LANES:(p + 1) * LANES] = piece[p].astype(F32)


def ungate(own, y, k, v, g, pieces):
    count = k.shape[0]
    step = count // NSEQ
    part = pl.BlockSpec((step, GROUP, LANES), lambda i: (i, 0, 0))
    lags = LENGTH // NSEQ
    return pl.pallas_call(
        ungate_kernel,
        grid=(NSEQ,),
        out_shape=(jax.ShapeDtypeStruct(k.shape, BF16),) * 3 + (jax.ShapeDtypeStruct((NSEQ * GROUP, lags), F32),),
        in_specs=[pl.BlockSpec(memory_space=pltpu.SMEM)] + [whole()] * 8,
        out_specs=(part,) * 3 + (pl.BlockSpec((GROUP, lags), lambda i: (i, 0)),),
        compiler_params=pltpu.CompilerParams(vmem_limit_bytes=24 * 2**20),
        name="ungate",
    )(own, y, k, v, g, *pieces)


def exchange_lags(corr, own):
    quarters = corr.reshape(NSEQ, BLOCKS // NSEQ, GROUP, LANES)
    got = [lax.dynamic_index_in_dim(quarters, own, 0, keepdims=False)]
    for shift in range(1, NSEQ):
        sent = lax.dynamic_index_in_dim(quarters, own ^ shift, 0, keepdims=False)
        got.append(lax.ppermute(sent, DP, [(d, d ^ shift) for d in range(NSEQ)]))
    return got


def exchange(array):
    flat = array.reshape((-1,) + array.shape[len(LEAD):])
    return lax.all_to_all(flat, ORDER, 0, 0, tiled=True).reshape(array.shape)


def shards(q_gate, k_gate, values, grad_out, filt):
    shape = q_gate.shape
    count = shape[1] // GROUP
    q, k, v, g = (a.reshape(count, GROUP, LANES) for a in (q_gate, k_gate, values, grad_out))
    own = lax.axis_index(DP)
    slot = own.reshape(1)
    x, k, v, g = gate(slot, k, v, q, g, filt.reshape(count, OCTETS, OCTET, LANES))
    y, corr = convolve(exchange(x))
    *grads, filter_grad = ungate(slot, exchange(y), k, v, g, exchange_lags(corr, own))
    return tuple(grad.reshape(shape) for grad in grads) + (filter_grad,)


def solution(mesh):
    split = Mesh(mesh.devices.reshape(tuple(SPLIT.values())), tuple(SPLIT))
    part = P(DP, None, CTX)
    return jax.shard_map(
        shards,
        mesh=split,
        in_specs=(part, part, part, part, P(None, CTX)),
        out_specs=(part, part, part, P(CTX, DP)),
        check_vma=False,
    )
```

time: 99.6 us -> 102 us (1.024)
  local copies, waits for them, and re-layouts: 3.86 us -> 9.01 us
  Pallas kernels: 15 us -> 12.2 us
  blocking collectives: 44.5 us -> 42.9 us
  starting transfers between devices: 9.09 us -> 10.2 us
    unnamed x20 -> x30, local copies, waits for them, and re-layouts: 3.83 us -> 8.98 us
    pallas_call x2, Pallas kernels: 12.5 us -> 9.68 us  [the longest x1 8.54 us: convolve(): pl.pallas_call(convolve_kernel, grid=(OCTETS // per,), out_shape=(pltpu.H...]
    all_to_all x1, blocking collectives: 44.5 us -> 42.9 us  [exchange(): return lax.all_to_all(flat, ORDER, 0, 0, tiled=True).reshape(array.shape)]
    all_to_all x1, starting transfers between devices: 4.85 us -> 6.07 us  [exchange(): return lax.all_to_all(flat, ORDER, 0, 0, tiled=True).reshape(array.shape)]
  transfers between devices with their start and end apart: 4 -> 4, of which waited for: 3 -> 2; matrix products, arithmetic and copies ran while one was open for 0% -> 0% of each run, Pallas kernels for 0% -> 0%
where the time goes in v3:
time: 102 us
  blocking collectives  42.9 us (42%)
  waiting for transfers between devices  26.6 us (26%)
  Pallas kernels  12.2 us (12%)
  starting transfers between devices  10.2 us (10%)
  local copies, waits for them, and re-layouts  9.01 us (9%)
    all_to_all x1, blocking collectives, exchange(): return lax.all_to_all(flat, ORDER, 0, 0, tiled=True).reshape(array.shape)  42.9 us
    ppermute x3, waiting for transfers between devices, exchange_lags(): got.append(lax.ppermute(sent, DP, [(d, d ^ shift) for d in range(NSEQ)]))  26.6 us
    unnamed x30, local copies, waits for them, and re-layouts  8.98 us
    pallas_call x1, Pallas kernels, convolve(): pl.pallas_call(convolve_kernel, grid=(OCTETS // per,), out_shape=(pltpu.H...  8.54 us
    all_to_all x1, starting transfers between devices, exchange(): return lax.all_to_all(flat, ORDER, 0, 0, tiled=True).reshape(array.shape)  6.07 us
    ppermute x3, starting transfers between devices, exchange_lags(): got.append(lax.ppermute(sent, DP, [(d, d ^ shift) for d in range(NSEQ)]))  4.09 us
    pallas_call x1, Pallas kernels, ungate(): pl.pallas_call(ungate_kernel, grid=(NSEQ,), out_shape=(jax.ShapeDtypeStru...  2.51 us
  transfers between devices with their start and end apart: 4, of which 2 were waited for; matrix products, arithmetic and copies ran while one was open for 0% of the time, Pallas kernels for 0%

profile of v3, /device:TPU:1, one launch (start us, length us, event | category | flops | bytes accessed | tf_op | source)
XLA Modules:
  0.0 101.6 jit_solution(4322217506674430349)
XLA Ops:
  0.6 1.6 %copy-done = f32[4096,128]{1,0:T(8,128)S(1)} copy-done((f32[4096,128]{1,0:T(8,128)S(1)}, f32[4096,128]{1,0:T(8,128)}, u32[]{:S(2)}) %copy-start) | copy-done | bytes 2097176
  2.2 1.2 %copy-done.1 = bf16[1,4096,128]{2,1,0:T(8,128)(2,1)S(1)} copy-done((bf16[1,4096,128]{2,1,0:T(8,128)(2,1)S(1)}, bf16[1,4096,128]{2,1,0:T(8,128)(2,1)}, u32[]{:S(2)}) %copy-start.1) | copy-done | bytes 1048600
  3.5 1.2 %copy-done.2 = bf16[1,4096,128]{2,1,0:T(8,128)(2,1)S(1)} copy-done((bf16[1,4096,128]{2,1,0:T(8,128)(2,1)S(1)}, bf16[1,4096,128]{2,1,0:T(8,128)(2,1)}, u32[]{:S(2)}) %copy-start.2) | copy-done | bytes 1048600
  4.7 1.2 %copy-done.3 = bf16[1,4096,128]{2,1,0:T(8,128)(2,1)S(1)} copy-done((bf16[1,4096,128]{2,1,0:T(8,128)(2,1)S(1)}, bf16[1,4096,128]{2,1,0:T(8,128)(2,1)}, u32[]{:S(2)}) %copy-start.3) | copy-done | bytes 1048600
  5.9 1.2 %copy-done.4 = bf16[1,4096,128]{2,1,0:T(8,128)(2,1)S(1)} copy-done((bf16[1,4096,128]{2,1,0:T(8,128)(2,1)S(1)}, bf16[1,4096,128]{2,1,0:T(8,128)(2,1)}, u32[]{:S(2)}) %copy-start.4) | copy-done | bytes 1048600
  7.1 1.1 %gate.1 = (bf16[2,2,4,2,4,9,8,128]{7,6,5,4,3,2,1,0:T(8,128)(2,1)S(1)}, bf16[128,32,128]{2,1,0:T(8,128)(2,1)S(1)}, bf16[128,32,128]{2,1,0:T(8,128)(2,1)S(1)}, bf16[128,32,128]{2,1,0:T(8,128)(2,1)S(1)}) custom-call(s32[1]{0:T(128)} %bitcast.own_ref, bf16[128,32,128]{2,1,0:T(8,128)(2,1)S(1)} %bitcast.26, bf16[128,32,128]{2,1,0:T(8,128)(2,1)S(1)} %bitcast.27, ...), custom_call_target="tpu_custom_call" | custom-call | tf_op jit(solution)/shard_map/gate/pallas_call | solution.py:192
  8.3 0.0 copy-start.5
  8.3 0.0 copy-start.9
  8.3 0.0 copy-start.10
  8.3 0.0 copy-start.11
  8.3 0.0 copy-start.12
  8.4 0.0 copy-start.13
  8.4 0.0 copy-start.14
  8.4 42.9 %all_to_all.10 = bf16[128,9,8,128]{3,2,1,0:T(8,128)(2,1)S(1)} all-to-all(bf16[128,9,8,128]{3,2,1,0:T(8,128)(2,1)S(1)} %bitcast.24), channel_id=1, replica_groups=mesh['zh'=2,'k'=2,'y'=4,'x'=4,'zl'=2] {'zl','zh','x','k','y'}, dimensions={0} | all-to-all | bytes 4718592 | tf_op jit(solution)/shard_map/all_to_all | solution.py:259
  51.3 8.5 %convolve.1 = (bf16[2,2,4,2,4,8,8,128]{7,6,5,4,3,2,1,0:T(8,128)(2,1)}, bf16[4,4,2,4,8,128]{5,4,3,2,1,0:T(8,128)(2,1)S(1)}) custom-call(bf16[2,2,4,2,4,9,8,128]{7,6,5,4,3,2,1,0:T(8,128)(2,1)S(1)} %bitcast.23, bf16[512,256]{1,0:T(8,128)(2,1)S(1)} %copy-done.12, f32[2,256,128]{2,1,0:T(8,128)S(1)} %copy-done.11, bf16[256,256]{1,0:T(8,128)(2,1)S(1)} %copy-done.14, ...), custom_call_target="tpu_custom_call" | custom-call | flops 10000000000 | bytes 5242880 | tf_op jit(solution)/shard_map/convolve/pallas_call | solution.py:134
  59.9 6.1 %all-to-all-start.1 = ((bf16[128,8,8,128]{3,2,1,0:T(8,128)(2,1)}), bf16[128,8,8,128]{3,2,1,0:T(8,128)(2,1)S(1)}, u32[]{:S(2)}, u32[]{:S(2)}) async-start(bf16[128,8,8,128]{3,2,1,0:T(8,128)(2,1)} %bitcast.31), calls=%async_computation.1 | async-start | bytes 4194304 | tf_op jit(solution)/shard_map/all_to_all | solution.py:259
  66.0 3.6 %collective-permute-start.2 = (bf16[8,32,128]{2,1,0:T(8,128)(2,1)S(1)}, bf16[8,32,128]{2,1,0:T(8,128)(2,1)S(1)}, u32[]{:S(2)}, u32[]{:S(2)}) collective-permute-start(bf16[8,32,128]{2,1,0:T(8,128)(2,1)S(1)} %get-tuple-element.24), channel_id=1, source_target_pairs={{0,96},{32,64},{64,32},{96,0},{1,97},{33,65},{65,33},{97,1},{2,98}... | collective-permute-start | bytes 196616 | tf_op jit(solution)/shard_map/ppermute | solution.py:253
  69.6 0.4 collective-permute-start.1
  70.0 0.1 collective-permute-start
  70.1 25.0 %collective-permute-done.2.r3_ref = bf16[8,32,128]{2,1,0:T(8,128)(2,1)S(1)} collective-permute-done((bf16[8,32,128]{2,1,0:T(8,128)(2,1)S(1)}, bf16[8,32,128]{2,1,0:T(8,128)(2,1)S(1)}, u32[]{:S(2)}, u32[]{:S(2)}) %collective-permute-start.2) | collective-permute-done | bytes 65568 | tf_op jit(solution)/shard_map/ppermute | solution.py:253
  95.1 1.5 %collective-permute-done.1.r2_ref = bf16[8,32,128]{2,1,0:T(8,128)(2,1)S(1)} collective-permute-done((bf16[8,32,128]{2,1,0:T(8,128)(2,1)S(1)}, bf16[8,32,128]{2,1,0:T(8,128)(2,1)S(1)}, u32[]{:S(2)}, u32[]{:S(2)}) %collective-permute-start.1) | collective-permute-done | bytes 65568 | tf_op jit(solution)/shard_map/ppermute | solution.py:253
  96.7 1.2 %copy-done.6 = bf16[128,32,128]{2,1,0:T(8,128)(2,1)S(1)} copy-done((bf16[128,32,128]{2,1,0:T(8,128)(2,1)S(1)}, bf16[128,32,128]{2,1,0:T(8,128)(2,1)}, u32[]{:S(2)}) %copy-start.6) | copy-done | bytes 1048600
  97.9 1.2 %copy-done.8 = bf16[128,32,128]{2,1,0:T(8,128)(2,1)S(1)} copy-done((bf16[128,32,128]{2,1,0:T(8,128)(2,1)S(1)}, bf16[128,32,128]{2,1,0:T(8,128)(2,1)}, u32[]{:S(2)}) %copy-start.8) | copy-done | bytes 1048600
  99.1 2.5 %ungate.1 = (bf16[128,32,128]{2,1,0:T(8,128)(2,1)}, bf16[128,32,128]{2,1,0:T(8,128)(2,1)}, bf16[128,32,128]{2,1,0:T(8,128)(2,1)}, f32[128,1024]{1,0:T(8,128)}) custom-call(s32[1]{0:T(128)} %bitcast.own_ref, bf16[2,2,4,2,4,8,8,128]{7,6,5,4,3,2,1,0:T(8,128)(2,1)S(1)} %bitcast.22, bf16[128,32,128]{2,1,0:T(8,128)(2,1)S(1)} %get-tuple-element.16.k_ref, ...), custom_call_target="tpu_custom_call" | custom-call | tf_op jit(solution)/shard_map/ungate/pallas_call | solution.py:237
  (19 shorter events, 0.1 us)
Async XLA Ops:
  0.6 1.6 %copy-start = (f32[4096,128]{1,0:T(8,128)S(1)}, f32[4096,128]{1,0:T(8,128)}, u32[]{:S(2)}) copy-start(f32[4096,128]{1,0:T(8,128)} %param.15) | copy-start | bytes 6291460
  2.2 1.2 %copy-start.1 = (bf16[1,4096,128]{2,1,0:T(8,128)(2,1)S(1)}, bf16[1,4096,128]{2,1,0:T(8,128)(2,1)}, u32[]{:S(2)}) copy-start(bf16[1,4096,128]{2,1,0:T(8,128)(2,1)} %param.12) | copy-start | bytes 3145732
  3.5 1.2 %copy-start.2 = (bf16[1,4096,128]{2,1,0:T(8,128)(2,1)S(1)}, bf16[1,4096,128]{2,1,0:T(8,128)(2,1)}, u32[]{:S(2)}) copy-start(bf16[1,4096,128]{2,1,0:T(8,128)(2,1)} %param.13) | copy-start | bytes 3145732
  4.7 1.2 %copy-start.3 = (bf16[1,4096,128]{2,1,0:T(8,128)(2,1)S(1)}, bf16[1,4096,128]{2,1,0:T(8,128)(2,1)}, u32[]{:S(2)}) copy-start(bf16[1,4096,128]{2,1,0:T(8,128)(2,1)} %param.11) | copy-start | bytes 3145732
  5.9 1.2 %copy-start.4 = (bf16[1,4096,128]{2,1,0:T(8,128)(2,1)S(1)}, bf16[1,4096,128]{2,1,0:T(8,128)(2,1)}, u32[]{:S(2)}) copy-start(bf16[1,4096,128]{2,1,0:T(8,128)(2,1)} %param.14) | copy-start | bytes 3145732
  8.3 43.0 %copy-start.5 = (bf16[128,32,128]{2,1,0:T(8,128)(2,1)}, bf16[128,32,128]{2,1,0:T(8,128)(2,1)S(1)}, u32[]{:S(2)}) copy-start(bf16[128,32,128]{2,1,0:T(8,128)(2,1)S(1)} %get-tuple-element.17.v_ref) | copy-start | bytes 3145732
  8.3 43.0 %copy-start.7 = (bf16[128,32,128]{2,1,0:T(8,128)(2,1)}, bf16[128,32,128]{2,1,0:T(8,128)(2,1)S(1)}, u32[]{:S(2)}) copy-start(bf16[128,32,128]{2,1,0:T(8,128)(2,1)S(1)} %get-tuple-element.18.g_ref) | copy-start | bytes 3145732
  8.3 43.0 %copy-start.9 = (bf16[256,512]{1,0:T(8,128)(2,1)S(1)}, bf16[256,512]{1,0:T(8,128)(2,1)}, u32[]{:S(2)}) copy-start(bf16[256,512]{1,0:T(8,128)(2,1)} %constant.45.clone.last_ref) | copy-start | bytes 786436
  8.3 43.0 %copy-start.10 = (f32[2,256,128]{2,1,0:T(8,128)S(1)}, f32[2,256,128]{2,1,0:T(8,128)}, u32[]{:S(2)}) copy-start(f32[2,256,128]{2,1,0:T(8,128)} %constant.44.clone.untwist_ref) | copy-start | bytes 786436
  8.3 43.0 %copy-start.11 = (f32[2,256,128]{2,1,0:T(8,128)S(1)}, f32[2,256,128]{2,1,0:T(8,128)}, u32[]{:S(2)}) copy-start(f32[2,256,128]{2,1,0:T(8,128)} %constant.41.clone.twist_ref) | copy-start | bytes 786436
  8.3 43.0 %copy-start.12 = (bf16[512,256]{1,0:T(8,128)(2,1)S(1)}, bf16[512,256]{1,0:T(8,128)(2,1)}, u32[]{:S(2)}) copy-start(bf16[512,256]{1,0:T(8,128)(2,1)} %constant.40.clone.first_ref) | copy-start | bytes 786436
  8.4 42.9 %copy-start.13 = (bf16[256,256]{1,0:T(8,128)(2,1)S(1)}, bf16[256,256]{1,0:T(8,128)(2,1)}, u32[]{:S(2)}) copy-start(bf16[256,256]{1,0:T(8,128)(2,1)} %constant.43.clone.inverse_ref) | copy-start | bytes 393220
  8.4 42.9 %copy-start.14 = (bf16[256,256]{1,0:T(8,128)(2,1)S(1)}, bf16[256,256]{1,0:T(8,128)(2,1)}, u32[]{:S(2)}) copy-start(bf16[256,256]{1,0:T(8,128)(2,1)} %constant.42.clone.second_ref) | copy-start | bytes 393220
  59.9 36.8 %all-to-all-start.1 = ((bf16[128,8,8,128]{3,2,1,0:T(8,128)(2,1)}), bf16[128,8,8,128]{3,2,1,0:T(8,128)(2,1)S(1)}, u32[]{:S(2)}, u32[]{:S(2)}) async-start(bf16[128,8,8,128]{3,2,1,0:T(8,128)(2,1)} %bitcast.31), calls=%async_computation.1 | async-start | bytes 4194304 | tf_op jit(solution)/shard_map/all_to_all | solution.py:259
  66.0 29.1 %collective-permute-start.2 = (bf16[8,32,128]{2,1,0:T(8,128)(2,1)S(1)}, bf16[8,32,128]{2,1,0:T(8,128)(2,1)S(1)}, u32[]{:S(2)}, u32[]{:S(2)}) collective-permute-start(bf16[8,32,128]{2,1,0:T(8,128)(2,1)S(1)} %get-tuple-element.24), channel_id=1, source_target_pairs={{0,96},{32,64},{64,32},{96,0},{1,97},{33,65},{65,33},{97,1},{2,98}... | collective-permute-start | bytes 196616 | tf_op jit(solution)/shard_map/ppermute | solution.py:253
  69.6 27.0 %collective-permute-start.1 = (bf16[8,32,128]{2,1,0:T(8,128)(2,1)S(1)}, bf16[8,32,128]{2,1,0:T(8,128)(2,1)S(1)}, u32[]{:S(2)}, u32[]{:S(2)}) collective-permute-start(bf16[8,32,128]{2,1,0:T(8,128)(2,1)S(1)} %get-tuple-element.25), channel_id=1, source_target_pairs={{0,64},{32,96},{64,0},{96,32},{1,65},{33,97},{65,1},{97,33},{2,66}... | collective-permute-start | bytes 196616 | tf_op jit(solution)/shard_map/ppermute | solution.py:253
  70.0 26.7 %collective-permute-start = (bf16[8,32,128]{2,1,0:T(8,128)(2,1)S(1)}, bf16[8,32,128]{2,1,0:T(8,128)(2,1)S(1)}, u32[]{:S(2)}, u32[]{:S(2)}) collective-permute-start(bf16[8,32,128]{2,1,0:T(8,128)(2,1)S(1)} %get-tuple-element.26), channel_id=1, source_target_pairs={{0,32},{32,0},{64,96},{96,64},{1,33},{33,1},{65,97},{97,65},{2,34}... | collective-permute-start | bytes 196616 | tf_op jit(solution)/shard_map/ppermute | solution.py:253
  96.7 1.2 %copy-start.6 = (bf16[128,32,128]{2,1,0:T(8,128)(2,1)S(1)}, bf16[128,32,128]{2,1,0:T(8,128)(2,1)}, u32[]{:S(2)}) copy-start(bf16[128,32,128]{2,1,0:T(8,128)(2,1)} %copy-done.5) | copy-start | bytes 3145732
  97.9 1.2 %copy-start.8 = (bf16[128,32,128]{2,1,0:T(8,128)(2,1)S(1)}, bf16[128,32,128]{2,1,0:T(8,128)(2,1)}, u32[]{:S(2)}) copy-start(bf16[128,32,128]{2,1,0:T(8,128)(2,1)} %copy-done.7) | copy-start | bytes 3145732

commit v4 on v3

--- a/solution.py
+++ b/solution.py
@@ -154,7 +154,7 @@
 
 
 def gate_kernel(
-    own_ref, k_ref, v_ref, q_ref, g_ref, filt_ref, x_out, k_in, v_in, g_in, q_in, filt_in, in_sem, filt_sem,
+    own_ref, k_ref, v_ref, q_ref, g_ref, filt_ref, x_out, k_in, v_in, q_in, g_in, filt_in, in_sem, filt_sem,
 ):
     parts = SPLIT["y"]
     step = k_in.shape[0] // parts
@@ -184,65 +184,105 @@
                 x_out[zl, zh, :, :, y, 2 * OCTETS] = lags[:, zl, zh].astype(BF16)
 
 
+def in_hbm(array):
+    return pltpu.with_memory_space_constraint(array, pltpu.HBM)
+
+
 def gate(own, k, v, q, g, filt):
     count = k.shape[0]
     parts = SPLIT["y"]
     far = pl.BlockSpec(memory_space=pltpu.HBM)
-    kept = jax.ShapeDtypeStruct(k.shape, BF16)
     return pl.pallas_call(
         gate_kernel,
-        out_shape=(jax.ShapeDtypeStruct(LEAD + (SIGNALS, OCTET, LANES), BF16), kept, kept, kept),
+        out_shape=jax.ShapeDtypeStruct(LEAD + (SIGNALS, OCTET, LANES), BF16),
         in_specs=[pl.BlockSpec(memory_space=pltpu.SMEM)] + [far] * 5,
-        out_specs=(whole(),) * 4,
-        scratch_shapes=[
-            pltpu.VMEM(k.shape, BF16),
+        out_specs=whole(),
+        scratch_shapes=[pltpu.VMEM(k.shape, BF16)] * 4
+        + [
             pltpu.VMEM((count, OCTET, LANES), F32),
             pltpu.SemaphoreType.DMA((parts, 4)),
             pltpu.SemaphoreType.DMA((parts,)),
         ],
         compiler_params=pltpu.CompilerParams(vmem_limit_bytes=24 * 2**20),
         name="gate",
-    )(own, k, v, q, g, filt)
-
-
-def ungate_kernel(own_ref, y_ref, k_ref, v_ref, g_ref, r0_ref, r1_ref, r2_ref, r3_ref, gq_ref, gk_ref, gv_ref, corr_ref):
-    i = pl.program_id(0)
-    step = gq_ref.shape[0]
-    for x in range(4):
-        for zl in range(2):
-            for zh in range(2):
-                row = x * 8 + zl * 4 + zh * 2
-                here, there = pl.ds(row, 2), pl.ds(i * step + row, 2)
-                conv, back = (
-                    jnp.concatenate([y_ref[zl, zh, x, :, i, 2 * j + part].astype(F32) for j in range(OCTETS)], axis=1)
-                    for part in range(2)
-                )
-                gq_ref[here] = product(g_ref[there], conv).astype(BF16)
-                gk_ref[here] = product(back, v_ref[there]).astype(BF16)
-                gv_ref[here] = product(back, k_ref[there]).astype(BF16)
-    source = i ^ own_ref[0]
-    for s, piece in enumerate((r0_ref, r1_ref, r2_ref, r3_ref)):
-
-        @pl.when(source == s)
-        def _(piece=piece):
-            for p in range(piece.shape[0]):
-                corr_ref[:, p * LANES:(p + 1) * LANES] = piece[p].astype(F32)
+    )(own, *(in_hbm(array) for array in (k, v, q, g, filt)))
+
+
+def ungate_kernel(
+    own_ref, y_ref, k_ref, v_ref, g_ref, r0_ref, r1_ref, r2_ref, r3_ref, gq_ref, gk_ref, gv_ref, corr_ref,
+    k_in, v_in, g_in, r_in, gq_out, gk_out, gv_out, corr_out, in_sem, r_sem, out_sem, corr_sem,
+):
+    parts = SPLIT["y"]
+    step = k_in.shape[0] // parts
+
+    def arrive(i):
+        at = pl.ds(i * step, step)
+        refs = ((k_ref, k_in), (v_ref, v_in), (g_ref, g_in))
+        return [pltpu.make_async_copy(a.at[at], b.at[at], in_sem.at[i, n]) for n, (a, b) in enumerate(refs)]
+
+    def leave(i):
+        at = pl.ds(i * step, step)
+        refs = ((gq_out, gq_ref), (gk_out, gk_ref), (gv_out, gv_ref))
+        return [pltpu.make_async_copy(a.at[at], b.at[at], out_sem.at[i, n]) for n, (a, b) in enumerate(refs)]
+
+    pieces = [pltpu.make_async_copy(r, r_in.at[s], r_sem.at[s]) for s, r in enumerate((r0_ref, r1_ref, r2_ref, r3_ref))]
+    for copy in pieces:
+        copy.start()
+    for i in range(parts):
+        for copy in arrive(i):
+            copy.start()
+    for s, copy in enumerate(pieces):
+        copy.wait()
+        rows = pl.ds(pl.multiple_of((own_ref[0] ^ s) * GROUP, GROUP), GROUP)
+        for p in range(BLOCKS // NSEQ):
+            corr_out[rows, p * LANES:(p + 1) * LANES] = r_in[s, p].astype(F32)
+    corr_copy = pltpu.make_async_copy(corr_out, corr_ref, corr_sem)
+    corr_copy.start()
+    for i in range(parts):
+        for copy in arrive(i):
+            copy.wait()
+        for x in range(4):
+            for zl in range(2):
+                for zh in range(2):
+                    at = pl.ds(i * step + x * 8 + zl * 4 + zh * 2, 2)
+                    conv, back = (
+                        jnp.concatenate([y_ref[zl, zh, x, :, i, 2 * j + part].astype(F32) for j in range(OCTETS)], axis=1)
+                        for part in range(2)
+                    )
+                    gq_out[at] = product(g_in[at], conv).astype(BF16)
+                    gk_out[at] = product(back, v_in[at]).astype(BF16)
+                    gv_out[at] = product(back, k_in[at]).astype(BF16)
+        for copy in leave(i):
+            copy.start()
+    for i in range(parts):
+        for copy in leave(i):
+            copy.wait()
+    corr_copy.wait()
 
 
 def ungate(own, y, k, v, g, pieces):
-    count = k.shape[0]
-    step = count // NSEQ
-    part = pl.BlockSpec((step, GROUP, LANES), lambda i: (i, 0, 0))
+    parts = SPLIT["y"]
     lags = LENGTH // NSEQ
+    far = pl.BlockSpec(memory_space=pltpu.HBM)
+    corr_shape = (NSEQ * GROUP, lags)
     return pl.pallas_call(
         ungate_kernel,
-        grid=(NSEQ,),
-        out_shape=(jax.ShapeDtypeStruct(k.shape, BF16),) * 3 + (jax.ShapeDtypeStruct((NSEQ * GROUP, lags), F32),),
-        in_specs=[pl.BlockSpec(memory_space=pltpu.SMEM)] + [whole()] * 8,
-        out_specs=(part,) * 3 + (pl.BlockSpec((GROUP, lags), lambda i: (i, 0)),),
+        out_shape=(pltpu.HBM(k.shape, BF16),) * 3 + (pltpu.HBM(corr_shape, F32),),
+        in_specs=[pl.BlockSpec(memory_space=pltpu.SMEM), whole()] + [far] * 7,
+        out_specs=(far,) * 4,
+        scratch_shapes=[pltpu.VMEM(k.shape, BF16)] * 3
+        + [pltpu.VMEM((NSEQ,) + pieces[0].shape, BF16)]
+        + [pltpu.VMEM(k.shape, BF16)] * 3
+        + [
+            pltpu.VMEM(corr_shape, F32),
+            pltpu.SemaphoreType.DMA((parts, 3)),
+            pltpu.SemaphoreType.DMA((NSEQ,)),
+            pltpu.SemaphoreType.DMA((parts, 3)),
+            pltpu.SemaphoreType.DMA,
+        ],
         compiler_params=pltpu.CompilerParams(vmem_limit_bytes=24 * 2**20),
         name="ungate",
-    )(own, y, k, v, g, *pieces)
+    )(own, y, *(in_hbm(array) for array in (k, v, g, *pieces)))
 
 
 def exchange_lags(corr, own):
@@ -265,9 +305,10 @@
     q, k, v, g = (a.reshape(count, GROUP, LANES) for a in (q_gate, k_gate, values, grad_out))
     own = lax.axis_index(DP)
     slot = own.reshape(1)
-    x, k, v, g = gate(slot, k, v, q, g, filt.reshape(count, OCTETS, OCTET, LANES))
+    x = gate(slot, k, v, q, g, filt.reshape(count, OCTETS, OCTET, LANES))
     y, corr = convolve(exchange(x))
-    *grads, filter_grad = ungate(slot, exchange(y), k, v, g, exchange_lags(corr, own))
+    pieces = exchange_lags(corr, own)
+    *grads, filter_grad = ungate(slot, exchange(y), k, v, g, pieces)
     return tuple(grad.reshape(shape) for grad in grads) + (filter_grad,)
 
 

time: 102 us -> 96.7 us (0.948)
  local copies, waits for them, and re-layouts: 9.01 us -> 1.32 us
  Pallas kernels: 12.2 us -> 15 us
    unnamed x30 -> x18, local copies, waits for them, and re-layouts: 8.98 us -> 0.68 us
    pallas_call x2, Pallas kernels: 3.65 us -> 6.47 us  [the longest x1 3.85 us: ungate(): pl.pallas_call(ungate_kernel, out_shape=(pltpu.HBM(k.shape, BF16),) * 3 +...]
  transfers between devices with their start and end apart: 4 -> 4, of which waited for: 2 -> 2; matrix products, arithmetic and copies ran while one was open for 0% -> 1% of each run, Pallas kernels for 0% -> 0%
where the time goes in v4:
time: 96.7 us; the launch traced here: 96.5 us
  blocking collectives  42.9 us (44%)
  waiting for transfers between devices  26.5 us (27%)
  Pallas kernels  15 us (16%)
  starting transfers between devices  10 us (10%)
  local copies, waits for them, and re-layouts  1.32 us (1%)
    all_to_all x1, blocking collectives, exchange(): return lax.all_to_all(flat, ORDER, 0, 0, tiled=True).reshape(array.shape)  42.9 us
    ppermute x3, waiting for transfers between devices, exchange_lags(): got.append(lax.ppermute(sent, DP, [(d, d ^ shift) for d in range(NSEQ)]))  26.5 us
    pallas_call x1, Pallas kernels, convolve(): pl.pallas_call(convolve_kernel, grid=(OCTETS // per,), out_shape=(pltpu.H...  8.52 us
    all_to_all x1, starting transfers between devices, exchange(): return lax.all_to_all(flat, ORDER, 0, 0, tiled=True).reshape(array.shape)  6.07 us
    ppermute x3, starting transfers between devices, exchange_lags(): got.append(lax.ppermute(sent, DP, [(d, d ^ shift) for d in range(NSEQ)]))  3.95 us
    pallas_call x1, Pallas kernels, ungate(): pl.pallas_call(ungate_kernel, out_shape=(pltpu.HBM(k.shape, BF16),) * 3 +...  3.85 us
    pallas_call x1, Pallas kernels, gate(): pl.pallas_call(gate_kernel, out_shape=jax.ShapeDtypeStruct(LEAD + (SIGNAL...  2.63 us
  transfers between devices with their start and end apart: 4, of which 2 were waited for; matrix products, arithmetic and copies ran while one was open for 1% of the time, Pallas kernels for 0%

profile of v4, /device:TPU:1, one launch (start us, length us, event | category | flops | bytes accessed | tf_op | source)
XLA Modules:
  0.0 96.5 jit_solution(17790701916756365262)
XLA Ops:
  0.6 2.6 %gate.1 = bf16[2,2,4,2,4,9,8,128]{7,6,5,4,3,2,1,0:T(8,128)(2,1)S(1)} custom-call(s32[1]{0:T(128)} %bitcast.own_ref, bf16[128,32,128]{2,1,0:T(8,128)(2,1)} %bitcast.26, bf16[128,32,128]{2,1,0:T(8,128)(2,1)} %bitcast.28, bf16[128,32,128]{2,1,0:T(8,128)(2,1)} %bitcast.34, bf16[128,32,128]{2,1,0:T(8,128)(2,1)} %bitcast.30, f32[128,4,8,128]{3,2,1,0:T(8,128)} %bitcast.32), custom_call_target="tpu_custom_call" | custom-call | tf_op jit(solution)/shard_map/gate/pallas_call | solution.py:195
  3.3 0.0 copy-start
  3.3 0.0 copy-start.1
  3.3 0.0 copy-start.2
  3.3 0.0 copy-start.3
  3.3 0.0 copy-start.4
  3.3 0.0 copy-start.5
  3.3 42.9 %all_to_all.10 = bf16[128,9,8,128]{3,2,1,0:T(8,128)(2,1)S(1)} all-to-all(bf16[128,9,8,128]{3,2,1,0:T(8,128)(2,1)S(1)} %bitcast.22), channel_id=1, replica_groups=mesh['zh'=2,'k'=2,'y'=4,'x'=4,'zl'=2] {'zl','zh','x','k','y'}, dimensions={0} | all-to-all | bytes 4718592 | tf_op jit(solution)/shard_map/all_to_all | solution.py:299
  46.2 0.0 copy-done
  46.2 0.0 copy-done.1
  46.2 0.0 copy-done.2
  46.3 8.5 %convolve.1 = (bf16[2,2,4,2,4,8,8,128]{7,6,5,4,3,2,1,0:T(8,128)(2,1)}, bf16[4,4,2,4,8,128]{5,4,3,2,1,0:T(8,128)(2,1)S(1)}) custom-call(bf16[2,2,4,2,4,9,8,128]{7,6,5,4,3,2,1,0:T(8,128)(2,1)S(1)} %bitcast.24, bf16[512,256]{1,0:T(8,128)(2,1)S(1)} %copy-done.3, f32[2,256,128]{2,1,0:T(8,128)S(1)} %copy-done.2, bf16[256,256]{1,0:T(8,128)(2,1)S(1)} %copy-done.5, ...), custom_call_target="tpu_custom_call" | custom-call | flops 10000000000 | bytes 5242880 | tf_op jit(solution)/shard_map/convolve/pallas_call | solution.py:134
  54.8 6.1 %all-to-all-start.1 = ((bf16[128,8,8,128]{3,2,1,0:T(8,128)(2,1)}), bf16[128,8,8,128]{3,2,1,0:T(8,128)(2,1)S(1)}, u32[]{:S(2)}, u32[]{:S(2)}) async-start(bf16[128,8,8,128]{3,2,1,0:T(8,128)(2,1)} %bitcast.33), calls=%async_computation.1 | async-start | bytes 4194304 | tf_op jit(solution)/shard_map/all_to_all | solution.py:299
  60.9 0.6 dynamic-slice_bitcast_fusion
  61.5 3.5 %collective-permute-start.2 = (bf16[8,32,128]{2,1,0:T(8,128)(2,1)S(1)}, bf16[8,32,128]{2,1,0:T(8,128)(2,1)S(1)}, u32[]{:S(2)}, u32[]{:S(2)}) collective-permute-start(bf16[8,32,128]{2,1,0:T(8,128)(2,1)S(1)} %get-tuple-element.16), channel_id=1, source_target_pairs={{0,96},{32,64},{64,32},{96,0},{1,97},{33,65},{65,33},{97,1},{2,98}... | collective-permute-start | bytes 196616 | tf_op jit(solution)/shard_map/ppermute | solution.py:293
  65.1 0.4 collective-permute-start.1
  65.4 0.0 collective-permute-start
  65.5 24.6 %collective-permute-done.2.r3_ref = bf16[8,32,128]{2,1,0:T(8,128)(2,1)S(1)} collective-permute-done((bf16[8,32,128]{2,1,0:T(8,128)(2,1)S(1)}, bf16[8,32,128]{2,1,0:T(8,128)(2,1)S(1)}, u32[]{:S(2)}, u32[]{:S(2)}) %collective-permute-start.2) | collective-permute-done | bytes 65568 | tf_op jit(solution)/shard_map/ppermute | solution.py:293
  90.1 1.9 %collective-permute-done.1.r2_ref = bf16[8,32,128]{2,1,0:T(8,128)(2,1)S(1)} collective-permute-done((bf16[8,32,128]{2,1,0:T(8,128)(2,1)S(1)}, bf16[8,32,128]{2,1,0:T(8,128)(2,1)S(1)}, u32[]{:S(2)}, u32[]{:S(2)}) %collective-permute-start.1) | collective-permute-done | bytes 65568 | tf_op jit(solution)/shard_map/ppermute | solution.py:293
  92.0 0.0 collective-permute-done.r1_ref
  92.0 0.0 all-to-all-done.1
  92.0 0.6 copy-done.7
  92.6 0.0 copy-done.8
  92.6 3.8 %ungate.1 = (bf16[128,32,128]{2,1,0:T(8,128)(2,1)}, bf16[128,32,128]{2,1,0:T(8,128)(2,1)}, bf16[128,32,128]{2,1,0:T(8,128)(2,1)}, f32[128,1024]{1,0:T(8,128)}) custom-call(s32[1]{0:T(128)} %bitcast.own_ref, bf16[2,2,4,2,4,8,8,128]{7,6,5,4,3,2,1,0:T(8,128)(2,1)S(1)} %bitcast.23, bf16[128,32,128]{2,1,0:T(8,128)(2,1)} %bitcast.27, ...), custom_call_target="tpu_custom_call" | custom-call | tf_op jit(solution)/shard_map/ungate/pallas_call | solution.py:268
  (7 shorter events, 0.0 us)
Async XLA Ops:
  3.3 43.0 %copy-start = (bf16[256,512]{1,0:T(8,128)(2,1)S(1)}, bf16[256,512]{1,0:T(8,128)(2,1)}, u32[]{:S(2)}) copy-start(bf16[256,512]{1,0:T(8,128)(2,1)} %constant.45.clone.last_ref) | copy-start | bytes 786436
  3.3 42.9 %copy-start.1 = (f32[2,256,128]{2,1,0:T(8,128)S(1)}, f32[2,256,128]{2,1,0:T(8,128)}, u32[]{:S(2)}) copy-start(f32[2,256,128]{2,1,0:T(8,128)} %constant.44.clone.untwist_ref) | copy-start | bytes 786436
  3.3 42.9 %copy-start.2 = (f32[2,256,128]{2,1,0:T(8,128)S(1)}, f32[2,256,128]{2,1,0:T(8,128)}, u32[]{:S(2)}) copy-start(f32[2,256,128]{2,1,0:T(8,128)} %constant.41.clone.twist_ref) | copy-start | bytes 786436
  3.3 42.9 %copy-start.3 = (bf16[512,256]{1,0:T(8,128)(2,1)S(1)}, bf16[512,256]{1,0:T(8,128)(2,1)}, u32[]{:S(2)}) copy-start(bf16[512,256]{1,0:T(8,128)(2,1)} %constant.40.clone.first_ref) | copy-start | bytes 786436
  3.3 42.9 %copy-start.4 = (bf16[256,256]{1,0:T(8,128)(2,1)S(1)}, bf16[256,256]{1,0:T(8,128)(2,1)}, u32[]{:S(2)}) copy-start(bf16[256,256]{1,0:T(8,128)(2,1)} %constant.43.clone.inverse_ref) | copy-start | bytes 393220
  3.3 42.9 %copy-start.5 = (bf16[256,256]{1,0:T(8,128)(2,1)S(1)}, bf16[256,256]{1,0:T(8,128)(2,1)}, u32[]{:S(2)}) copy-start(bf16[256,256]{1,0:T(8,128)(2,1)} %constant.42.clone.second_ref) | copy-start | bytes 393220
  54.8 37.2 %all-to-all-start.1 = ((bf16[128,8,8,128]{3,2,1,0:T(8,128)(2,1)}), bf16[128,8,8,128]{3,2,1,0:T(8,128)(2,1)S(1)}, u32[]{:S(2)}, u32[]{:S(2)}) async-start(bf16[128,8,8,128]{3,2,1,0:T(8,128)(2,1)} %bitcast.33), calls=%async_computation.1 | async-start | bytes 4194304 | tf_op jit(solution)/shard_map/all_to_all | solution.py:299
  61.5 28.5 %collective-permute-start.2 = (bf16[8,32,128]{2,1,0:T(8,128)(2,1)S(1)}, bf16[8,32,128]{2,1,0:T(8,128)(2,1)S(1)}, u32[]{:S(2)}, u32[]{:S(2)}) collective-permute-start(bf16[8,32,128]{2,1,0:T(8,128)(2,1)S(1)} %get-tuple-element.16), channel_id=1, source_target_pairs={{0,96},{32,64},{64,32},{96,0},{1,97},{33,65},{65,33},{97,1},{2,98}... | collective-permute-start | bytes 196616 | tf_op jit(solution)/shard_map/ppermute | solution.py:293
  65.1 26.9 %collective-permute-start.1 = (bf16[8,32,128]{2,1,0:T(8,128)(2,1)S(1)}, bf16[8,32,128]{2,1,0:T(8,128)(2,1)S(1)}, u32[]{:S(2)}, u32[]{:S(2)}) collective-permute-start(bf16[8,32,128]{2,1,0:T(8,128)(2,1)S(1)} %get-tuple-element.17), channel_id=1, source_target_pairs={{0,64},{32,96},{64,0},{96,32},{1,65},{33,97},{65,1},{97,33},{2,66}... | collective-permute-start | bytes 196616 | tf_op jit(solution)/shard_map/ppermute | solution.py:293
  65.4 26.5 %collective-permute-start = (bf16[8,32,128]{2,1,0:T(8,128)(2,1)S(1)}, bf16[8,32,128]{2,1,0:T(8,128)(2,1)S(1)}, u32[]{:S(2)}, u32[]{:S(2)}) collective-permute-start(bf16[8,32,128]{2,1,0:T(8,128)(2,1)S(1)} %get-tuple-element.18), channel_id=1, source_target_pairs={{0,32},{32,0},{64,96},{96,64},{1,33},{33,1},{65,97},{97,65},{2,34}... | collective-permute-start | bytes 196616 | tf_op jit(solution)/shard_map/ppermute | solution.py:293
  90.1 1.9 %copy-start.6 = (bf16[8,32,128]{2,1,0:T(8,128)(2,1)}, bf16[8,32,128]{2,1,0:T(8,128)(2,1)S(1)}, u32[]{:S(2)}) copy-start(bf16[8,32,128]{2,1,0:T(8,128)(2,1)S(1)} %collective-permute-done.2.r3_ref) | copy-start | bytes 196612
  92.0 0.6 copy-start.7
  92.0 0.6 copy-start.8

commit v5 on v4

--- a/solution.py
+++ b/solution.py
@@ -63,40 +63,49 @@
     return jnp.concatenate([real, imag], axis=1).astype(BF16)
 
 
-def octet(signals, first, twist, second, inverse, untwist, last):
+def octets(groups, first, twist, second, inverse, untwist, last):
+    count = len(groups)
+    gated = SIGNALS - 1
+    signals = [signal for group in groups for signal in group[:gated]] + [group[gated] for group in groups]
+
+    def index(o, s):
+        return o * gated + s if s < gated else count * gated + o
+
     spectra = []
-    for s in range(0, SIGNALS, 2):
-        both = signals[s:s + 2]
-        width = len(both) * LANES
-        part = dot(first, jnp.concatenate(both, axis=1)).reshape(BLOCKS, 2, OCTET, width)
-        real, imag = part[:, 0].reshape(ROWS, width), part[:, 1].reshape(ROWS, width)
-        for at in range(0, width, LANES):
+    for s in range(0, len(signals), 2):
+        part = dot(first, jnp.concatenate(signals[s:s + 2], axis=1)).reshape(BLOCKS, 2, OCTET, 2 * LANES)
+        real, imag = part[:, 0].reshape(ROWS, 2 * LANES), part[:, 1].reshape(ROWS, 2 * LANES)
+        for at in range(0, 2 * LANES, LANES):
             line = pair(*turn_by(real[:, at:at + LANES], imag[:, at:at + LANES], *twist))
             spectrum = dot(line, second)
             spectra.append((spectrum[:, :LANES], spectrum[:, LANES:]))
-    filt_real, filt_imag = spectra[2 * NSEQ]
-    convs, backs = [], []
-    corr_real = corr_imag = None
-    for n in range(NSEQ):
-        in_real, in_imag = spectra[n]
-        grad_real, grad_imag = spectra[NSEQ + n]
-        convs.append(pair(*turn_by(in_real, in_imag, filt_real, filt_imag)))
-        backs.append(pair(grad_real * filt_real + grad_imag * filt_imag, grad_imag * filt_real - grad_real * filt_imag))
-        real = grad_real * in_real + grad_imag * in_imag
-        imag = grad_imag * in_real - grad_real * in_imag
-        corr_real = real if corr_real is None else corr_real + real
-        corr_imag = imag if corr_imag is None else corr_imag + imag
-    columns = []
-    for product_spectrum in convs + backs + [pair(corr_real, corr_imag)]:
-        line = dot(product_spectrum, inverse)
-        real, imag = turn_by(line[:, :LANES], line[:, LANES:], *untwist)
-        mixed = jnp.stack([real.reshape(BLOCKS, OCTET, LANES), imag.reshape(BLOCKS, OCTET, LANES)], axis=1)
-        columns.append(mixed.reshape(2 * ROWS, LANES).astype(BF16))
+    products = [None] * len(signals)
+    for o in range(count):
+        filt_real, filt_imag = spectra[index(o, gated)]
+        corr_real = corr_imag = None
+        for n in range(NSEQ):
+            in_real, in_imag = spectra[index(o, n)]
+            grad_real, grad_imag = spectra[index(o, NSEQ + n)]
+            products[index(o, n)] = pair(*turn_by(in_real, in_imag, filt_real, filt_imag))
+            products[index(o, NSEQ + n)] = pair(
+                grad_real * filt_real + grad_imag * filt_imag, grad_imag * filt_real - grad_real * filt_imag
+            )
+            real = grad_real * in_real + grad_imag * in_imag
+            imag = grad_imag * in_real - grad_real * in_imag
+            corr_real = real if corr_real is None else corr_real + real
+            corr_imag = imag if corr_imag is None else corr_imag + imag
+        products[index(o, gated)] = pair(corr_real, corr_imag)
     results = []
-    for s in range(0, SIGNALS, 2):
-        out = dot(last, jnp.concatenate(columns[s:s + 2], axis=1))
-        results += [out[:, at:at + LANES] for at in range(0, out.shape[1], LANES)]
-    return results
+    for s in range(0, len(signals), 2):
+        columns = []
+        for spectrum in products[s:s + 2]:
+            line = dot(spectrum, inverse)
+            real, imag = turn_by(line[:, :LANES], line[:, LANES:], *untwist)
+            mixed = jnp.stack([real.reshape(BLOCKS, OCTET, LANES), imag.reshape(BLOCKS, OCTET, LANES)], axis=1)
+            columns.append(mixed.reshape(2 * ROWS, LANES).astype(BF16))
+        out = dot(last, jnp.concatenate(columns, axis=1))
+        results += [out[:, :LANES], out[:, LANES:]]
+    return [[results[index(o, s)] for s in range(SIGNALS)] for o in range(count)]
 
 
 def convolve_kernel(
@@ -107,14 +116,16 @@
     def rows_of(piece):
         return piece.astype(F32).reshape(ROWS, LANES).astype(BF16)
 
+    groups = []
     for o in range(SPLIT["k"]):
         j = step * SPLIT["k"] + o
         signals = [rows_of(x_ref[:, n // 2, :, n % 2, :, 2 * j + part]) for part in range(2) for n in range(NSEQ)]
-        signals.append(rows_of(x_ref[:, step, :, o, :, 2 * OCTETS]))
-        out = octet(
-            signals, first_ref[...], (twist_ref[0], twist_ref[1]), second_ref[...], inverse_ref[...],
-            (untwist_ref[0], untwist_ref[1]), last_ref[...],
-        )
+        groups.append(signals + [rows_of(x_ref[:, step, :, o, :, 2 * OCTETS])])
+    results = octets(
+        groups, first_ref[...], (twist_ref[0], twist_ref[1]), second_ref[...], inverse_ref[...],
+        (untwist_ref[0], untwist_ref[1]), last_ref[...],
+    )
+    for o, out in enumerate(results):
         out = [piece.reshape(2, 4, 4, OCTET, LANES).astype(BF16) for piece in out]
         for n in range(NSEQ):
             for part in range(2):
@@ -209,8 +220,7 @@
 
 
 def ungate_kernel(
-    own_ref, y_ref, k_ref, v_ref, g_ref, r0_ref, r1_ref, r2_ref, r3_ref, gq_ref, gk_ref, gv_ref, corr_ref,
-    k_in, v_in, g_in, r_in, gq_out, gk_out, gv_out, corr_out, in_sem, r_sem, out_sem, corr_sem,
+    y_ref, k_ref, v_ref, g_ref, gq_ref, gk_ref, gv_ref, k_in, v_in, g_in, gq_out, gk_out, gv_out, in_sem, out_sem,
 ):
     parts = SPLIT["y"]
     step = k_in.shape[0] // parts
@@ -225,19 +235,9 @@
         refs = ((gq_out, gq_ref), (gk_out, gk_ref), (gv_out, gv_ref))
         return [pltpu.make_async_copy(a.at[at], b.at[at], out_sem.at[i, n]) for n, (a, b) in enumerate(refs)]
 
-    pieces = [pltpu.make_async_copy(r, r_in.at[s], r_sem.at[s]) for s, r in enumerate((r0_ref, r1_ref, r2_ref, r3_ref))]
-    for copy in pieces:
-        copy.start()
     for i in range(parts):
         for copy in arrive(i):
             copy.start()
-    for s, copy in enumerate(pieces):
-        copy.wait()
-        rows = pl.ds(pl.multiple_of((own_ref[0] ^ s) * GROUP, GROUP), GROUP)
-        for p in range(BLOCKS // NSEQ):
-            corr_out[rows, p * LANES:(p + 1) * LANES] = r_in[s, p].astype(F32)
-    corr_copy = pltpu.make_async_copy(corr_out, corr_ref, corr_sem)
-    corr_copy.start()
     for i in range(parts):
         for copy in arrive(i):
             copy.wait()
@@ -257,32 +257,47 @@
     for i in range(parts):
         for copy in leave(i):
             copy.wait()
-    corr_copy.wait()
-
-
-def ungate(own, y, k, v, g, pieces):
+
+
+def ungate(y, k, v, g):
     parts = SPLIT["y"]
-    lags = LENGTH // NSEQ
     far = pl.BlockSpec(memory_space=pltpu.HBM)
-    corr_shape = (NSEQ * GROUP, lags)
     return pl.pallas_call(
         ungate_kernel,
-        out_shape=(pltpu.HBM(k.shape, BF16),) * 3 + (pltpu.HBM(corr_shape, F32),),
-        in_specs=[pl.BlockSpec(memory_space=pltpu.SMEM), whole()] + [far] * 7,
-        out_specs=(far,) * 4,
-        scratch_shapes=[pltpu.VMEM(k.shape, BF16)] * 3
-        + [pltpu.VMEM((NSEQ,) + pieces[0].shape, BF16)]
-        + [pltpu.VMEM(k.shape, BF16)] * 3
-        + [
-            pltpu.VMEM(corr_shape, F32),
-            pltpu.SemaphoreType.DMA((parts, 3)),
-            pltpu.SemaphoreType.DMA((NSEQ,)),
-            pltpu.SemaphoreType.DMA((parts, 3)),
-            pltpu.SemaphoreType.DMA,
-        ],
+        out_shape=(pltpu.HBM(k.shape, BF16),) * 3,
+        in_specs=[whole()] + [far] * 3,
+        out_specs=(far,) * 3,
+        scratch_shapes=[pltpu.VMEM(k.shape, BF16)] * 6 + [pltpu.SemaphoreType.DMA((parts, 3))] * 2,
         compiler_params=pltpu.CompilerParams(vmem_limit_bytes=24 * 2**20),
+        cost_estimate=pl.CostEstimate(flops=0, bytes_accessed=8 * 2**20, transcendentals=0),
         name="ungate",
-    )(own, y, *(in_hbm(array) for array in (k, v, g, *pieces)))
+    )(y, *(in_hbm(array) for array in (k, v, g)))
+
+
+def gather_kernel(own_ref, after_ref, r0_ref, r1_ref, r2_ref, r3_ref, corr_ref, corr_out, sem):
+    del after_ref
+    copies = []
+    for s, piece in enumerate((r0_ref, r1_ref, r2_ref, r3_ref)):
+        rows = pl.ds(pl.multiple_of((own_ref[0] ^ s) * GROUP, GROUP), GROUP)
+        for p in range(BLOCKS // NSEQ):
+            corr_out[s, :, p * LANES:(p + 1) * LANES] = piece[p].astype(F32)
+        copies.append(pltpu.make_async_copy(corr_out.at[s], corr_ref.at[rows], sem.at[s]))
+        copies[-1].start()
+    for copy in copies:
+        copy.wait()
+
+
+def gather(own, after, pieces):
+    lags = LENGTH // NSEQ
+    return pl.pallas_call(
+        gather_kernel,
+        out_shape=pltpu.HBM((NSEQ * GROUP, lags), F32),
+        in_specs=[pl.BlockSpec(memory_space=pltpu.SMEM), pl.BlockSpec(memory_space=pltpu.HBM)] + [whole()] * NSEQ,
+        out_specs=pl.BlockSpec(memory_space=pltpu.HBM),
+        scratch_shapes=[pltpu.VMEM((NSEQ, GROUP, lags), F32), pltpu.SemaphoreType.DMA((NSEQ,))],
+        compiler_params=pltpu.CompilerParams(vmem_limit_bytes=16 * 2**20),
+        name="gather",
+    )(own, in_hbm(after), *pieces)
 
 
 def exchange_lags(corr, own):
@@ -308,7 +323,8 @@
     x = gate(slot, k, v, q, g, filt.reshape(count, OCTETS, OCTET, LANES))
     y, corr = convolve(exchange(x))
     pieces = exchange_lags(corr, own)
-    *grads, filter_grad = ungate(slot, exchange(y), k, v, g, pieces)
+    grads = ungate(exchange(y), k, v, g)
+    filter_grad = gather(slot, grads[0], pieces)
     return tuple(grad.reshape(shape) for grad in grads) + (filter_grad,)
 
 

time: 96.7 us -> 92.5 us (0.957)
  waiting for transfers between devices: 26.5 us -> 24.7 us
  local copies, waits for them, and re-layouts: 1.32 us -> 0.07 us
  Pallas kernels: 15 us -> 13.8 us
    ppermute x3, waiting for transfers between devices: 26.5 us -> 0.01 us  [exchange_lags(): got.append(lax.ppermute(sent, DP, [(d, d ^ shift) for d in range(NSEQ)]))]
    all_to_all x1, waiting for transfers between devices: 0.01 us -> 24.6 us  [exchange(): return lax.all_to_all(flat, ORDER, 0, 0, tiled=True).reshape(array.shape)]
    pallas_call x1, Pallas kernels: 8.52 us -> 7.27 us  [convolve(): pl.pallas_call(convolve_kernel, grid=(OCTETS // per,), out_shape=(pltpu.H...]
    pallas_call x1 -> x2, Pallas kernels: 3.85 us -> 3.86 us  [the longest x1 3.03 us: ungate(): pl.pallas_call(ungate_kernel, out_shape=(pltpu.HBM(k.shape, BF16),) * 3,...]
  transfers between devices with their start and end apart: 4 -> 4, of which waited for: 2 -> 1; matrix products, arithmetic and copies ran while one was open for 1% -> 0% of each run, Pallas kernels for 0% -> 3%
where the time goes in v5:
time: 92.5 us; the launch traced here: 92.3 us
  blocking collectives  42.9 us (46%)
  waiting for transfers between devices  24.7 us (27%)
  Pallas kernels  13.8 us (15%)
  starting transfers between devices  10.2 us (11%)
    all_to_all x1, blocking collectives, exchange(): return lax.all_to_all(flat, ORDER, 0, 0, tiled=True).reshape(array.shape)  42.9 us
    all_to_all x1, waiting for transfers between devices, exchange(): return lax.all_to_all(flat, ORDER, 0, 0, tiled=True).reshape(array.shape)  24.6 us
    pallas_call x1, Pallas kernels, convolve(): pl.pallas_call(convolve_kernel, grid=(OCTETS // per,), out_shape=(pltpu.H...  7.27 us
    all_to_all x1, starting transfers between devices, exchange(): return lax.all_to_all(flat, ORDER, 0, 0, tiled=True).reshape(array.shape)  6.08 us
    ppermute x3, starting transfers between devices, exchange_lags(): got.append(lax.ppermute(sent, DP, [(d, d ^ shift) for d in range(NSEQ)]))  4.09 us
    pallas_call x1, Pallas kernels, ungate(): pl.pallas_call(ungate_kernel, out_shape=(pltpu.HBM(k.shape, BF16),) * 3,...  3.03 us
    pallas_call x1, Pallas kernels, gate(): pl.pallas_call(gate_kernel, out_shape=jax.ShapeDtypeStruct(LEAD + (SIGNAL...  2.63 us
  transfers between devices with their start and end apart: 4, of which 1 were waited for; matrix products, arithmetic and copies ran while one was open for 0% of the time, Pallas kernels for 3%

profile of v5, /device:TPU:1, one launch (start us, length us, event | category | flops | bytes accessed | tf_op | source)
XLA Modules:
  0.0 92.3 jit_solution(870074833359638399)
XLA Ops:
  0.6 2.6 %gate.1 = bf16[2,2,4,2,4,9,8,128]{7,6,5,4,3,2,1,0:T(8,128)(2,1)S(1)} custom-call(s32[1]{0:T(128)} %bitcast.own_ref, bf16[128,32,128]{2,1,0:T(8,128)(2,1)} %bitcast.26, bf16[128,32,128]{2,1,0:T(8,128)(2,1)} %bitcast.28, bf16[128,32,128]{2,1,0:T(8,128)(2,1)} %bitcast.34, bf16[128,32,128]{2,1,0:T(8,128)(2,1)} %bitcast.30, f32[128,4,8,128]{3,2,1,0:T(8,128)} %bitcast.32), custom_call_target="tpu_custom_call" | custom-call | tf_op jit(solution)/shard_map/gate/pallas_call | solution.py:206
  3.3 0.0 copy-start
  3.3 0.0 copy-start.1
  3.3 0.0 copy-start.2
  3.3 0.0 copy-start.3
  3.3 0.0 copy-start.4
  3.3 0.0 copy-start.5
  3.3 42.9 %all_to_all.10 = bf16[128,9,8,128]{3,2,1,0:T(8,128)(2,1)S(1)} all-to-all(bf16[128,9,8,128]{3,2,1,0:T(8,128)(2,1)S(1)} %bitcast.22), channel_id=1, replica_groups=mesh['zh'=2,'k'=2,'y'=4,'x'=4,'zl'=2] {'zl','zh','x','k','y'}, dimensions={0} | all-to-all | bytes 4718592 | tf_op jit(solution)/shard_map/all_to_all | solution.py:314
  46.2 0.0 copy-done
  46.2 0.0 copy-done.1
  46.2 0.0 copy-done.2
  46.2 0.0 copy-done.3
  46.2 0.0 copy-done.4
  46.3 7.3 %convolve.1 = (bf16[2,2,4,2,4,8,8,128]{7,6,5,4,3,2,1,0:T(8,128)(2,1)}, bf16[4,4,2,4,8,128]{5,4,3,2,1,0:T(8,128)(2,1)S(1)}) custom-call(bf16[2,2,4,2,4,9,8,128]{7,6,5,4,3,2,1,0:T(8,128)(2,1)S(1)} %bitcast.24, bf16[512,256]{1,0:T(8,128)(2,1)S(1)} %copy-done.3, f32[2,256,128]{2,1,0:T(8,128)S(1)} %copy-done.2, bf16[256,256]{1,0:T(8,128)(2,1)S(1)} %copy-done.5, ...), custom_call_target="tpu_custom_call" | custom-call | flops 10000000000 | bytes 5242880 | tf_op jit(solution)/shard_map/convolve/pallas_call | solution.py:145
  53.5 6.1 %all-to-all-start.1 = ((bf16[128,8,8,128]{3,2,1,0:T(8,128)(2,1)}), bf16[128,8,8,128]{3,2,1,0:T(8,128)(2,1)S(1)}, u32[]{:S(2)}, u32[]{:S(2)}) async-start(bf16[128,8,8,128]{3,2,1,0:T(8,128)(2,1)} %bitcast.33), calls=%async_computation.1 | async-start | bytes 4194304 | tf_op jit(solution)/shard_map/all_to_all | solution.py:314
  59.7 3.6 %collective-permute-start.2 = (bf16[8,32,128]{2,1,0:T(8,128)(2,1)S(1)}, bf16[8,32,128]{2,1,0:T(8,128)(2,1)S(1)}, u32[]{:S(2)}, u32[]{:S(2)}) collective-permute-start(bf16[8,32,128]{2,1,0:T(8,128)(2,1)S(1)} %get-tuple-element.14), channel_id=1, source_target_pairs={{0,96},{32,64},{64,32},{96,0},{1,97},{33,65},{65,33},{97,1},{2,98}... | collective-permute-start | bytes 196616 | tf_op jit(solution)/shard_map/ppermute | solution.py:308
  63.3 0.4 collective-permute-start.1
  63.7 0.1 collective-permute-start
  63.8 24.6 %all-to-all-done.1 = bf16[128,8,8,128]{3,2,1,0:T(8,128)(2,1)S(1)} async-done(((bf16[128,8,8,128]{3,2,1,0:T(8,128)(2,1)}), bf16[128,8,8,128]{3,2,1,0:T(8,128)(2,1)S(1)}, u32[]{:S(2)}, u32[]{:S(2)}) %all-to-all-start.1) | async-done | bytes 2097184 | tf_op jit(solution)/shard_map/all_to_all | solution.py:314
  88.4 3.0 %ungate.1 = (bf16[128,32,128]{2,1,0:T(8,128)(2,1)}, bf16[128,32,128]{2,1,0:T(8,128)(2,1)}, bf16[128,32,128]{2,1,0:T(8,128)(2,1)}) custom-call(bf16[2,2,4,2,4,8,8,128]{7,6,5,4,3,2,1,0:T(8,128)(2,1)S(1)} %bitcast.23, bf16[128,32,128]{2,1,0:T(8,128)(2,1)} %bitcast.27, bf16[128,32,128]{2,1,0:T(8,128)(2,1)} %bitcast.29, bf16[128,32,128]{2,1,0:T(8,128)(2,1)} %bitcast.31), custom_call_target="tpu_custom_call" | custom-call | bytes 8388608 | tf_op jit(solution)/shard_map/ungate/pallas_call | solution.py:265
  91.4 0.0 collective-permute-done.2.r3_ref
  91.4 0.0 collective-permute-done.1.r2_ref
  91.5 0.0 collective-permute-done.r1_ref
  91.5 0.8 gather.1
  (2 shorter events, 0.0 us)
Async XLA Ops:
  3.3 43.0 %copy-start = (bf16[256,512]{1,0:T(8,128)(2,1)S(1)}, bf16[256,512]{1,0:T(8,128)(2,1)}, u32[]{:S(2)}) copy-start(bf16[256,512]{1,0:T(8,128)(2,1)} %constant.45.clone.last_ref) | copy-start | bytes 786436
  3.3 42.9 %copy-start.1 = (f32[2,256,128]{2,1,0:T(8,128)S(1)}, f32[2,256,128]{2,1,0:T(8,128)}, u32[]{:S(2)}) copy-start(f32[2,256,128]{2,1,0:T(8,128)} %constant.44.clone.untwist_ref) | copy-start | bytes 786436
  3.3 42.9 %copy-start.2 = (f32[2,256,128]{2,1,0:T(8,128)S(1)}, f32[2,256,128]{2,1,0:T(8,128)}, u32[]{:S(2)}) copy-start(f32[2,256,128]{2,1,0:T(8,128)} %constant.41.clone.twist_ref) | copy-start | bytes 786436
  3.3 42.9 %copy-start.3 = (bf16[512,256]{1,0:T(8,128)(2,1)S(1)}, bf16[512,256]{1,0:T(8,128)(2,1)}, u32[]{:S(2)}) copy-start(bf16[512,256]{1,0:T(8,128)(2,1)} %constant.40.clone.first_ref) | copy-start | bytes 786436
  3.3 42.9 %copy-start.4 = (bf16[256,256]{1,0:T(8,128)(2,1)S(1)}, bf16[256,256]{1,0:T(8,128)(2,1)}, u32[]{:S(2)}) copy-start(bf16[256,256]{1,0:T(8,128)(2,1)} %constant.43.clone.inverse_ref) | copy-start | bytes 393220
  3.3 42.9 %copy-start.5 = (bf16[256,256]{1,0:T(8,128)(2,1)S(1)}, bf16[256,256]{1,0:T(8,128)(2,1)}, u32[]{:S(2)}) copy-start(bf16[256,256]{1,0:T(8,128)(2,1)} %constant.42.clone.second_ref) | copy-start | bytes 393220
  53.5 34.9 %all-to-all-start.1 = ((bf16[128,8,8,128]{3,2,1,0:T(8,128)(2,1)}), bf16[128,8,8,128]{3,2,1,0:T(8,128)(2,1)S(1)}, u32[]{:S(2)}, u32[]{:S(2)}) async-start(bf16[128,8,8,128]{3,2,1,0:T(8,128)(2,1)} %bitcast.33), calls=%async_computation.1 | async-start | bytes 4194304 | tf_op jit(solution)/shard_map/all_to_all | solution.py:314
  59.7 31.8 %collective-permute-start.2 = (bf16[8,32,128]{2,1,0:T(8,128)(2,1)S(1)}, bf16[8,32,128]{2,1,0:T(8,128)(2,1)S(1)}, u32[]{:S(2)}, u32[]{:S(2)}) collective-permute-start(bf16[8,32,128]{2,1,0:T(8,128)(2,1)S(1)} %get-tuple-element.14), channel_id=1, source_target_pairs={{0,96},{32,64},{64,32},{96,0},{1,97},{33,65},{65,33},{97,1},{2,98}... | collective-permute-start | bytes 196616 | tf_op jit(solution)/shard_map/ppermute | solution.py:308
  63.3 28.2 %collective-permute-start.1 = (bf16[8,32,128]{2,1,0:T(8,128)(2,1)S(1)}, bf16[8,32,128]{2,1,0:T(8,128)(2,1)S(1)}, u32[]{:S(2)}, u32[]{:S(2)}) collective-permute-start(bf16[8,32,128]{2,1,0:T(8,128)(2,1)S(1)} %get-tuple-element.15), channel_id=1, source_target_pairs={{0,64},{32,96},{64,0},{96,32},{1,65},{33,97},{65,1},{97,33},{2,66}... | collective-permute-start | bytes 196616 | tf_op jit(solution)/shard_map/ppermute | solution.py:308
  63.7 27.8 %collective-permute-start = (bf16[8,32,128]{2,1,0:T(8,128)(2,1)S(1)}, bf16[8,32,128]{2,1,0:T(8,128)(2,1)S(1)}, u32[]{:S(2)}, u32[]{:S(2)}) collective-permute-start(bf16[8,32,128]{2,1,0:T(8,128)(2,1)S(1)} %get-tuple-element.16), channel_id=1, source_target_pairs={{0,32},{32,0},{64,96},{96,64},{1,33},{33,1},{65,97},{97,65},{2,34}... | collective-permute-start | bytes 196616 | tf_op jit(solution)/shard_map/ppermute | solution.py:308

commit v6 on v5

--- a/solution.py
+++ b/solution.py
@@ -22,13 +22,27 @@
 
 SPLIT = {"zh": 2, "k": 2, "y": 4, "x": 4, "zl": 2}
 DP, CTX = ("zh", "k"), ("y", "x", "zl")
-ORDER = ("zl", "zh", "x", "k", "y")
-LEAD = tuple(SPLIT[axis] for axis in ORDER)
+GO = ("zl", "zh", "x", "k", "y")
+BACK = ("k", "zh", "zl", "x", "y")
+GO_LEAD, BACK_LEAD = (tuple(SPLIT[axis] for axis in order) for order in (GO, BACK))
+
+
+def place(order, **at):
+    return tuple(at.get(axis, slice(None)) for axis in order)
+
+
+def taken(order):
+    axes = [axis for axis in order if axis in CTX]
+    weight = {"y": SPLIT["x"] * SPLIT["zl"], "x": SPLIT["zl"], "zl": 1}
+    blocks = np.zeros((), int)
+    for axis in axes:
+        blocks = blocks[..., None] + weight[axis] * np.arange(SPLIT[axis])
+    return [int(block) for block in blocks.reshape(-1)]
 
 
 def make_tables():
     rows = np.arange(BLOCKS) + 0.5
-    block = np.array([y * 8 + x * 2 + zl for zl in range(2) for x in range(4) for y in range(4)])
+    block = np.arange(BLOCKS)
     lane = np.arange(LANES)
     eye = np.eye(OCTET)
     phase = 2.0 * math.pi * rows[:, None] * block[None, :] / (2 * BLOCKS)
@@ -42,12 +56,12 @@
     second = np.block([[cosine, -sine], [sine, cosine]])
     inverse = np.block([[cosine, sine], [-sine, cosine]])
     return (
-        np.kron(first, eye).astype(jnp.bfloat16),
+        np.kron(first[:, taken(GO)], eye).astype(jnp.bfloat16),
         twist.astype(np.float32),
         second.astype(jnp.bfloat16),
         inverse.astype(jnp.bfloat16),
         untwist.astype(np.float32),
-        np.kron(first.T, eye).astype(jnp.bfloat16),
+        np.kron(first[:, taken(BACK)].T, eye).astype(jnp.bfloat16),
     )
 
 
@@ -112,6 +126,7 @@
     x_ref, first_ref, twist_ref, second_ref, inverse_ref, untwist_ref, last_ref, y_ref, corr_ref,
 ):
     step = pl.program_id(0)
+    back = tuple(SPLIT[axis] for axis in BACK if axis in CTX)
 
     def rows_of(piece):
         return piece.astype(F32).reshape(ROWS, LANES).astype(BF16)
@@ -119,20 +134,20 @@
     groups = []
     for o in range(SPLIT["k"]):
         j = step * SPLIT["k"] + o
-        signals = [rows_of(x_ref[:, n // 2, :, n % 2, :, 2 * j + part]) for part in range(2) for n in range(NSEQ)]
-        groups.append(signals + [rows_of(x_ref[:, step, :, o, :, 2 * OCTETS])])
+        signals = [rows_of(x_ref[place(GO, zh=n // 2, k=n % 2) + (2 * j + part,)]) for part in range(2) for n in range(NSEQ)]
+        groups.append(signals + [rows_of(x_ref[place(GO, zh=step, k=o) + (2 * OCTETS,)])])
     results = octets(
         groups, first_ref[...], (twist_ref[0], twist_ref[1]), second_ref[...], inverse_ref[...],
         (untwist_ref[0], untwist_ref[1]), last_ref[...],
     )
     for o, out in enumerate(results):
-        out = [piece.reshape(2, 4, 4, OCTET, LANES).astype(BF16) for piece in out]
+        out = [piece.reshape(BLOCKS, OCTET, LANES).astype(BF16) for piece in out]
         for n in range(NSEQ):
             for part in range(2):
-                y_ref[:, n // 2, :, n % 2, :, 2 * o + part] = out[part * NSEQ + n]
-        for zl in range(2):
-            for x in range(4):
-                corr_ref[:, x, zl, o] = out[2 * NSEQ][zl, x]
+                at = place(BACK, zh=n // 2, k=n % 2) + (2 * o + part,)
+                y_ref[at] = out[part * NSEQ + n].reshape(back + (OCTET, LANES))
+        for at, block in enumerate(taken(BACK)):
+            corr_ref[block, o] = out[2 * NSEQ][at]
 
 
 def whole():
@@ -146,13 +161,13 @@
         convolve_kernel,
         grid=(OCTETS // per,),
         out_shape=(
-            pltpu.HBM(LEAD + (2 * OCTETS, OCTET, LANES), BF16),
-            jax.ShapeDtypeStruct((4, 4, 2, OCTETS, OCTET, LANES), BF16),
+            pltpu.HBM(BACK_LEAD + (2 * OCTETS, OCTET, LANES), BF16),
+            jax.ShapeDtypeStruct((BLOCKS, OCTETS, OCTET, LANES), BF16),
         ),
         in_specs=[whole()] * (1 + len(tables)),
         out_specs=(
-            pl.BlockSpec(LEAD + (2 * per, OCTET, LANES), lambda j: (0, 0, 0, 0, 0, j, 0, 0)),
-            pl.BlockSpec((4, 4, 2, per, OCTET, LANES), lambda j: (0, 0, 0, j, 0, 0)),
+            pl.BlockSpec(BACK_LEAD + (2 * per, OCTET, LANES), lambda j: (0, 0, 0, 0, 0, j, 0, 0)),
+            pl.BlockSpec((BLOCKS, per, OCTET, LANES), lambda j: (0, j, 0, 0)),
         ),
         compiler_params=pltpu.CompilerParams(vmem_limit_bytes=44 * 2**20),
         cost_estimate=pl.CostEstimate(flops=10**10, bytes_accessed=5 * 2**20, transcendentals=0),
@@ -188,11 +203,13 @@
         lags = filt_in[at].reshape(4, 2, 2, 2, OCTET, LANES)
         for zl in range(2):
             for zh in range(2):
-                for j in range(OCTETS):
-                    rows = slice(j * OCTET, (j + 1) * OCTET)
-                    x_out[zl, zh, :, :, y, 2 * j] = mixed[:, zl, zh, :, rows].astype(BF16)
-                    x_out[zl, zh, :, :, y, 2 * j + 1] = grad_mix[:, zl, zh, :, rows].astype(BF16)
-                x_out[zl, zh, :, :, y, 2 * OCTETS] = lags[:, zl, zh].astype(BF16)
+                for k in range(2):
+                    at = place(GO, zl=zl, zh=zh, k=k, y=y)
+                    for j in range(OCTETS):
+                        rows = slice(j * OCTET, (j + 1) * OCTET)
+                        x_out[at + (2 * j,)] = mixed[:, zl, zh, k, rows].astype(BF16)
+                        x_out[at + (2 * j + 1,)] = grad_mix[:, zl, zh, k, rows].astype(BF16)
+                    x_out[at + (2 * OCTETS,)] = lags[:, zl, zh, k].astype(BF16)
 
 
 def in_hbm(array):
@@ -205,7 +222,7 @@
     far = pl.BlockSpec(memory_space=pltpu.HBM)
     return pl.pallas_call(
         gate_kernel,
-        out_shape=jax.ShapeDtypeStruct(LEAD + (SIGNALS, OCTET, LANES), BF16),
+        out_shape=jax.ShapeDtypeStruct(GO_LEAD + (SIGNALS, OCTET, LANES), BF16),
         in_specs=[pl.BlockSpec(memory_space=pltpu.SMEM)] + [far] * 5,
         out_specs=whole(),
         scratch_shapes=[pltpu.VMEM(k.shape, BF16)] * 4
@@ -245,8 +262,9 @@
             for zl in range(2):
                 for zh in range(2):
                     at = pl.ds(i * step + x * 8 + zl * 4 + zh * 2, 2)
+                    from_ = place(BACK, zl=zl, zh=zh, x=x, y=i)
                     conv, back = (
-                        jnp.concatenate([y_ref[zl, zh, x, :, i, 2 * j + part].astype(F32) for j in range(OCTETS)], axis=1)
+                        jnp.concatenate([y_ref[from_ + (2 * j + part,)].astype(F32) for j in range(OCTETS)], axis=1)
                         for part in range(2)
                     )
                     gq_out[at] = product(g_in[at], conv).astype(BF16)
@@ -309,9 +327,9 @@
     return got
 
 
-def exchange(array):
-    flat = array.reshape((-1,) + array.shape[len(LEAD):])
-    return lax.all_to_all(flat, ORDER, 0, 0, tiled=True).reshape(array.shape)
+def exchange(array, order):
+    flat = array.reshape((-1,) + array.shape[len(order):])
+    return lax.all_to_all(flat, order, 0, 0, tiled=True).reshape(array.shape)
 
 
 def shards(q_gate, k_gate, values, grad_out, filt):
@@ -321,9 +339,9 @@
     own = lax.axis_index(DP)
     slot = own.reshape(1)
     x = gate(slot, k, v, q, g, filt.reshape(count, OCTETS, OCTET, LANES))
-    y, corr = convolve(exchange(x))
+    y, corr = convolve(exchange(x, GO))
     pieces = exchange_lags(corr, own)
-    grads = ungate(exchange(y), k, v, g)
+    grads = ungate(exchange(y, BACK), k, v, g)
     filter_grad = gather(slot, grads[0], pieces)
     return tuple(grad.reshape(shape) for grad in grads) + (filter_grad,)
 

time: 92.5 us -> 92.3 us (level)
  no operation moved by 1% of the time
where the time goes in v6:
time: 92.3 us; the launch traced here: 92.1 us
  blocking collectives  42.9 us (46%)
  waiting for transfers between devices  24.4 us (26%)
  Pallas kernels  13.7 us (15%)
  starting transfers between devices  10.2 us (11%)
    all_to_all x1, blocking collectives, exchange(): return lax.all_to_all(flat, order, 0, 0, tiled=True).reshape(array.shape)  42.9 us
    all_to_all x1, waiting for transfers between devices, exchange(): return lax.all_to_all(flat, order, 0, 0, tiled=True).reshape(array.shape)  24.4 us
    pallas_call x1, Pallas kernels, convolve(): pl.pallas_call(convolve_kernel, grid=(OCTETS // per,), out_shape=(pltpu.H...  7.27 us
    all_to_all x1, starting transfers between devices, exchange(): return lax.all_to_all(flat, order, 0, 0, tiled=True).reshape(array.shape)  6.08 us
    ppermute x3, starting transfers between devices, exchange_lags(): got.append(lax.ppermute(sent, DP, [(d, d ^ shift) for d in range(NSEQ)]))  4.09 us
    pallas_call x1, Pallas kernels, ungate(): pl.pallas_call(ungate_kernel, out_shape=(pltpu.HBM(k.shape, BF16),) * 3,...  3.03 us
    pallas_call x1, Pallas kernels, gate(): pl.pallas_call(gate_kernel, out_shape=jax.ShapeDtypeStruct(GO_LEAD + (SIG...  2.63 us
  transfers between devices with their start and end apart: 4, of which 1 were waited for; matrix products, arithmetic and copies ran while one was open for 0% of the time, Pallas kernels for 3%

profile of v6, /device:TPU:1, one launch (start us, length us, event | category | flops | bytes accessed | tf_op | source)
XLA Modules:
  0.0 92.1 jit_solution(10628818673417559723)
XLA Ops:
  0.6 2.6 %gate.1 = bf16[2,2,4,2,4,9,8,128]{7,6,5,4,3,2,1,0:T(8,128)(2,1)S(1)} custom-call(s32[1]{0:T(128)} %bitcast.own_ref, bf16[128,32,128]{2,1,0:T(8,128)(2,1)} %bitcast.26, bf16[128,32,128]{2,1,0:T(8,128)(2,1)} %bitcast.28, bf16[128,32,128]{2,1,0:T(8,128)(2,1)} %bitcast.34, bf16[128,32,128]{2,1,0:T(8,128)(2,1)} %bitcast.30, f32[128,4,8,128]{3,2,1,0:T(8,128)} %bitcast.32), custom_call_target="tpu_custom_call" | custom-call | tf_op jit(solution)/shard_map/gate/pallas_call | solution.py:223
  3.3 0.0 copy-start
  3.3 0.0 copy-start.1
  3.3 0.0 copy-start.2
  3.3 0.0 copy-start.3
  3.3 0.0 copy-start.4
  3.3 0.0 copy-start.5
  3.3 42.9 %all_to_all.10 = bf16[128,9,8,128]{3,2,1,0:T(8,128)(2,1)S(1)} all-to-all(bf16[128,9,8,128]{3,2,1,0:T(8,128)(2,1)S(1)} %bitcast.22), channel_id=1, replica_groups=mesh['zh'=2,'k'=2,'y'=4,'x'=4,'zl'=2] {'zl','zh','x','k','y'}, dimensions={0} | all-to-all | bytes 4718592 | tf_op jit(solution)/shard_map/all_to_all | solution.py:332
  46.2 0.0 copy-done
  46.2 0.0 copy-done.1
  46.2 0.0 copy-done.3
  46.2 0.0 copy-done.4
  46.3 0.0 copy-done.5
  46.3 7.3 %convolve.1 = (bf16[2,2,2,4,4,8,8,128]{7,6,5,4,3,2,1,0:T(8,128)(2,1)}, bf16[32,4,8,128]{3,2,1,0:T(8,128)(2,1)S(1)}) custom-call(bf16[2,2,4,2,4,9,8,128]{7,6,5,4,3,2,1,0:T(8,128)(2,1)S(1)} %bitcast.24, bf16[512,256]{1,0:T(8,128)(2,1)S(1)} %copy-done.3, f32[2,256,128]{2,1,0:T(8,128)S(1)} %copy-done.2, bf16[256,256]{1,0:T(8,128)(2,1)S(1)} %copy-done.5, ...), custom_call_target="tpu_custom_call" | custom-call | flops 10000000000 | bytes 5242880 | tf_op jit(solution)/shard_map/convolve/pallas_call | solution.py:160
  53.5 6.1 %all-to-all-start.1 = ((bf16[128,8,8,128]{3,2,1,0:T(8,128)(2,1)}), bf16[128,8,8,128]{3,2,1,0:T(8,128)(2,1)S(1)}, u32[]{:S(2)}, u32[]{:S(2)}) async-start(bf16[128,8,8,128]{3,2,1,0:T(8,128)(2,1)} %bitcast.33), calls=%async_computation.1 | async-start | bytes 4194304 | tf_op jit(solution)/shard_map/all_to_all | solution.py:332
  59.7 3.6 %collective-permute-start.2 = (bf16[8,32,128]{2,1,0:T(8,128)(2,1)S(1)}, bf16[8,32,128]{2,1,0:T(8,128)(2,1)S(1)}, u32[]{:S(2)}, u32[]{:S(2)}) collective-permute-start(bf16[8,32,128]{2,1,0:T(8,128)(2,1)S(1)} %get-tuple-element.14), channel_id=1, source_target_pairs={{0,96},{32,64},{64,32},{96,0},{1,97},{33,65},{65,33},{97,1},{2,98}... | collective-permute-start | bytes 196616 | tf_op jit(solution)/shard_map/ppermute | solution.py:326
  63.3 0.4 collective-permute-start.1
  63.7 0.1 collective-permute-start
  63.8 24.4 %all-to-all-done.1 = bf16[128,8,8,128]{3,2,1,0:T(8,128)(2,1)S(1)} async-done(((bf16[128,8,8,128]{3,2,1,0:T(8,128)(2,1)}), bf16[128,8,8,128]{3,2,1,0:T(8,128)(2,1)S(1)}, u32[]{:S(2)}, u32[]{:S(2)}) %all-to-all-start.1) | async-done | bytes 2097184 | tf_op jit(solution)/shard_map/all_to_all | solution.py:332
  88.2 3.0 %ungate.1 = (bf16[128,32,128]{2,1,0:T(8,128)(2,1)}, bf16[128,32,128]{2,1,0:T(8,128)(2,1)}, bf16[128,32,128]{2,1,0:T(8,128)(2,1)}) custom-call(bf16[2,2,2,4,4,8,8,128]{7,6,5,4,3,2,1,0:T(8,128)(2,1)S(1)} %bitcast.23, bf16[128,32,128]{2,1,0:T(8,128)(2,1)} %bitcast.27, bf16[128,32,128]{2,1,0:T(8,128)(2,1)} %bitcast.29, bf16[128,32,128]{2,1,0:T(8,128)(2,1)} %bitcast.31), custom_call_target="tpu_custom_call" | custom-call | bytes 8388608 | tf_op jit(solution)/shard_map/ungate/pallas_call | solution.py:283
  91.2 0.0 collective-permute-done.2.r3_ref
  91.2 0.0 collective-permute-done.1.r2_ref
  91.2 0.0 collective-permute-done.r1_ref
  91.2 0.8 gather.1
  (2 shorter events, 0.0 us)
Async XLA Ops:
  3.3 43.0 %copy-start = (bf16[256,512]{1,0:T(8,128)(2,1)S(1)}, bf16[256,512]{1,0:T(8,128)(2,1)}, u32[]{:S(2)}) copy-start(bf16[256,512]{1,0:T(8,128)(2,1)} %constant.45.clone.last_ref) | copy-start | bytes 786436
  3.3 42.9 %copy-start.1 = (f32[2,256,128]{2,1,0:T(8,128)S(1)}, f32[2,256,128]{2,1,0:T(8,128)}, u32[]{:S(2)}) copy-start(f32[2,256,128]{2,1,0:T(8,128)} %constant.44.clone.untwist_ref) | copy-start | bytes 786436
  3.3 42.9 %copy-start.2 = (f32[2,256,128]{2,1,0:T(8,128)S(1)}, f32[2,256,128]{2,1,0:T(8,128)}, u32[]{:S(2)}) copy-start(f32[2,256,128]{2,1,0:T(8,128)} %constant.41.clone.twist_ref) | copy-start | bytes 786436
  3.3 42.9 %copy-start.3 = (bf16[512,256]{1,0:T(8,128)(2,1)S(1)}, bf16[512,256]{1,0:T(8,128)(2,1)}, u32[]{:S(2)}) copy-start(bf16[512,256]{1,0:T(8,128)(2,1)} %constant.40.clone.first_ref) | copy-start | bytes 786436
  3.3 42.9 %copy-start.4 = (bf16[256,256]{1,0:T(8,128)(2,1)S(1)}, bf16[256,256]{1,0:T(8,128)(2,1)}, u32[]{:S(2)}) copy-start(bf16[256,256]{1,0:T(8,128)(2,1)} %constant.43.clone.inverse_ref) | copy-start | bytes 393220
  3.3 42.9 %copy-start.5 = (bf16[256,256]{1,0:T(8,128)(2,1)S(1)}, bf16[256,256]{1,0:T(8,128)(2,1)}, u32[]{:S(2)}) copy-start(bf16[256,256]{1,0:T(8,128)(2,1)} %constant.42.clone.second_ref) | copy-start | bytes 393220
  53.5 34.7 %all-to-all-start.1 = ((bf16[128,8,8,128]{3,2,1,0:T(8,128)(2,1)}), bf16[128,8,8,128]{3,2,1,0:T(8,128)(2,1)S(1)}, u32[]{:S(2)}, u32[]{:S(2)}) async-start(bf16[128,8,8,128]{3,2,1,0:T(8,128)(2,1)} %bitcast.33), calls=%async_computation.1 | async-start | bytes 4194304 | tf_op jit(solution)/shard_map/all_to_all | solution.py:332
  59.7 31.6 %collective-permute-start.2 = (bf16[8,32,128]{2,1,0:T(8,128)(2,1)S(1)}, bf16[8,32,128]{2,1,0:T(8,128)(2,1)S(1)}, u32[]{:S(2)}, u32[]{:S(2)}) collective-permute-start(bf16[8,32,128]{2,1,0:T(8,128)(2,1)S(1)} %get-tuple-element.14), channel_id=1, source_target_pairs={{0,96},{32,64},{64,32},{96,0},{1,97},{33,65},{65,33},{97,1},{2,98}... | collective-permute-start | bytes 196616 | tf_op jit(solution)/shard_map/ppermute | solution.py:326
  63.3 28.0 %collective-permute-start.1 = (bf16[8,32,128]{2,1,0:T(8,128)(2,1)S(1)}, bf16[8,32,128]{2,1,0:T(8,128)(2,1)S(1)}, u32[]{:S(2)}, u32[]{:S(2)}) collective-permute-start(bf16[8,32,128]{2,1,0:T(8,128)(2,1)S(1)} %get-tuple-element.15), channel_id=1, source_target_pairs={{0,64},{32,96},{64,0},{96,32},{1,65},{33,97},{65,1},{97,33},{2,66}... | collective-permute-start | bytes 196616 | tf_op jit(solution)/shard_map/ppermute | solution.py:326
  63.7 27.6 %collective-permute-start = (bf16[8,32,128]{2,1,0:T(8,128)(2,1)S(1)}, bf16[8,32,128]{2,1,0:T(8,128)(2,1)S(1)}, u32[]{:S(2)}, u32[]{:S(2)}) collective-permute-start(bf16[8,32,128]{2,1,0:T(8,128)(2,1)S(1)} %get-tuple-element.16), channel_id=1, source_target_pairs={{0,32},{32,0},{64,96},{96,64},{1,33},{33,1},{65,97},{97,65},{2,34}... | collective-permute-start | bytes 196616 | tf_op jit(solution)/shard_map/ppermute | solution.py:326

commit v7 on v6

--- a/solution.py
+++ b/solution.py
@@ -292,17 +292,12 @@
     )(y, *(in_hbm(array) for array in (k, v, g)))
 
 
-def gather_kernel(own_ref, after_ref, r0_ref, r1_ref, r2_ref, r3_ref, corr_ref, corr_out, sem):
+def gather_kernel(own_ref, after_ref, r0_ref, r1_ref, r2_ref, r3_ref, corr_ref):
     del after_ref
-    copies = []
     for s, piece in enumerate((r0_ref, r1_ref, r2_ref, r3_ref)):
         rows = pl.ds(pl.multiple_of((own_ref[0] ^ s) * GROUP, GROUP), GROUP)
         for p in range(BLOCKS // NSEQ):
-            corr_out[s, :, p * LANES:(p + 1) * LANES] = piece[p].astype(F32)
-        copies.append(pltpu.make_async_copy(corr_out.at[s], corr_ref.at[rows], sem.at[s]))
-        copies[-1].start()
-    for copy in copies:
-        copy.wait()
+            corr_ref[rows, p * LANES:(p + 1) * LANES] = piece[p].astype(F32)
 
 
 def gather(own, after, pieces):
@@ -311,8 +306,7 @@
         gather_kernel,
         out_shape=pltpu.HBM((NSEQ * GROUP, lags), F32),
         in_specs=[pl.BlockSpec(memory_space=pltpu.SMEM), pl.BlockSpec(memory_space=pltpu.HBM)] + [whole()] * NSEQ,
-        out_specs=pl.BlockSpec(memory_space=pltpu.HBM),
-        scratch_shapes=[pltpu.VMEM((NSEQ, GROUP, lags), F32), pltpu.SemaphoreType.DMA((NSEQ,))],
+        out_specs=pl.BlockSpec((NSEQ * GROUP, lags), lambda: (0, 0)),
         compiler_params=pltpu.CompilerParams(vmem_limit_bytes=16 * 2**20),
         name="gather",
     )(own, in_hbm(after), *pieces)

time: 92.3 us -> 92.3 us (level)
  no operation moved by 1% of the time
where the time goes in v7:
time: 92.3 us; the launch traced here: 92.1 us
  blocking collectives  42.9 us (46%)
  waiting for transfers between devices  24.4 us (26%)
  Pallas kernels  13.8 us (15%)
  starting transfers between devices  10.2 us (11%)
    all_to_all x1, blocking collectives, exchange(): return lax.all_to_all(flat, order, 0, 0, tiled=True).reshape(array.shape)  42.9 us
    all_to_all x1, waiting for transfers between devices, exchange(): return lax.all_to_all(flat, order, 0, 0, tiled=True).reshape(array.shape)  24.4 us
    pallas_call x1, Pallas kernels, convolve(): pl.pallas_call(convolve_kernel, grid=(OCTETS // per,), out_shape=(pltpu.H...  7.27 us
    all_to_all x1, starting transfers between devices, exchange(): return lax.all_to_all(flat, order, 0, 0, tiled=True).reshape(array.shape)  6.08 us
    ppermute x3, starting transfers between devices, exchange_lags(): got.append(lax.ppermute(sent, DP, [(d, d ^ shift) for d in range(NSEQ)]))  4.09 us
    pallas_call x1, Pallas kernels, ungate(): pl.pallas_call(ungate_kernel, out_shape=(pltpu.HBM(k.shape, BF16),) * 3,...  3.03 us
    pallas_call x1, Pallas kernels, gate(): pl.pallas_call(gate_kernel, out_shape=jax.ShapeDtypeStruct(GO_LEAD + (SIG...  2.63 us
  transfers between devices with their start and end apart: 4, of which 1 were waited for; matrix products, arithmetic and copies ran while one was open for 0% of the time, Pallas kernels for 3%

profile of v7, /device:TPU:1, one launch (start us, length us, event | category | flops | bytes accessed | tf_op | source)
XLA Modules:
  0.0 92.1 jit_solution(5107058827475858486)
XLA Ops:
  0.6 2.6 %gate.1 = bf16[2,2,4,2,4,9,8,128]{7,6,5,4,3,2,1,0:T(8,128)(2,1)S(1)} custom-call(s32[1]{0:T(128)} %bitcast.own_ref, bf16[128,32,128]{2,1,0:T(8,128)(2,1)} %bitcast.26, bf16[128,32,128]{2,1,0:T(8,128)(2,1)} %bitcast.28, bf16[128,32,128]{2,1,0:T(8,128)(2,1)} %bitcast.34, bf16[128,32,128]{2,1,0:T(8,128)(2,1)} %bitcast.30, f32[128,4,8,128]{3,2,1,0:T(8,128)} %bitcast.32), custom_call_target="tpu_custom_call" | custom-call | tf_op jit(solution)/shard_map/gate/pallas_call | solution.py:223
  3.3 0.0 copy-start
  3.3 0.0 copy-start.1
  3.3 0.0 copy-start.2
  3.3 0.0 copy-start.3
  3.3 0.0 copy-start.4
  3.3 0.0 copy-start.5
  3.3 42.9 %all_to_all.10 = bf16[128,9,8,128]{3,2,1,0:T(8,128)(2,1)S(1)} all-to-all(bf16[128,9,8,128]{3,2,1,0:T(8,128)(2,1)S(1)} %bitcast.22), channel_id=1, replica_groups=mesh['zh'=2,'k'=2,'y'=4,'x'=4,'zl'=2] {'zl','zh','x','k','y'}, dimensions={0} | all-to-all | bytes 4718592 | tf_op jit(solution)/shard_map/all_to_all | solution.py:326
  46.2 0.0 copy-done
  46.2 0.0 copy-done.1
  46.2 0.0 copy-done.2
  46.2 0.0 copy-done.3
  46.2 0.0 copy-done.4
  46.3 7.3 %convolve.1 = (bf16[2,2,2,4,4,8,8,128]{7,6,5,4,3,2,1,0:T(8,128)(2,1)}, bf16[32,4,8,128]{3,2,1,0:T(8,128)(2,1)S(1)}) custom-call(bf16[2,2,4,2,4,9,8,128]{7,6,5,4,3,2,1,0:T(8,128)(2,1)S(1)} %bitcast.24, bf16[512,256]{1,0:T(8,128)(2,1)S(1)} %copy-done.3, f32[2,256,128]{2,1,0:T(8,128)S(1)} %copy-done.2, bf16[256,256]{1,0:T(8,128)(2,1)S(1)} %copy-done.5, ...), custom_call_target="tpu_custom_call" | custom-call | flops 10000000000 | bytes 5242880 | tf_op jit(solution)/shard_map/convolve/pallas_call | solution.py:160
  53.5 6.1 %all-to-all-start.1 = ((bf16[128,8,8,128]{3,2,1,0:T(8,128)(2,1)}), bf16[128,8,8,128]{3,2,1,0:T(8,128)(2,1)S(1)}, u32[]{:S(2)}, u32[]{:S(2)}) async-start(bf16[128,8,8,128]{3,2,1,0:T(8,128)(2,1)} %bitcast.33), calls=%async_computation.1 | async-start | bytes 4194304 | tf_op jit(solution)/shard_map/all_to_all | solution.py:326
  59.7 3.6 %collective-permute-start.2 = (bf16[8,32,128]{2,1,0:T(8,128)(2,1)S(1)}, bf16[8,32,128]{2,1,0:T(8,128)(2,1)S(1)}, u32[]{:S(2)}, u32[]{:S(2)}) collective-permute-start(bf16[8,32,128]{2,1,0:T(8,128)(2,1)S(1)} %get-tuple-element.14), channel_id=1, source_target_pairs={{0,96},{32,64},{64,32},{96,0},{1,97},{33,65},{65,33},{97,1},{2,98}... | collective-permute-start | bytes 196616 | tf_op jit(solution)/shard_map/ppermute | solution.py:320
  63.3 0.4 collective-permute-start.1
  63.7 0.1 collective-permute-start
  63.8 24.4 %all-to-all-done.1 = bf16[128,8,8,128]{3,2,1,0:T(8,128)(2,1)S(1)} async-done(((bf16[128,8,8,128]{3,2,1,0:T(8,128)(2,1)}), bf16[128,8,8,128]{3,2,1,0:T(8,128)(2,1)S(1)}, u32[]{:S(2)}, u32[]{:S(2)}) %all-to-all-start.1) | async-done | bytes 2097184 | tf_op jit(solution)/shard_map/all_to_all | solution.py:326
  88.2 3.0 %ungate.1 = (bf16[128,32,128]{2,1,0:T(8,128)(2,1)}, bf16[128,32,128]{2,1,0:T(8,128)(2,1)}, bf16[128,32,128]{2,1,0:T(8,128)(2,1)}) custom-call(bf16[2,2,2,4,4,8,8,128]{7,6,5,4,3,2,1,0:T(8,128)(2,1)S(1)} %bitcast.23, bf16[128,32,128]{2,1,0:T(8,128)(2,1)} %bitcast.27, bf16[128,32,128]{2,1,0:T(8,128)(2,1)} %bitcast.29, bf16[128,32,128]{2,1,0:T(8,128)(2,1)} %bitcast.31), custom_call_target="tpu_custom_call" | custom-call | bytes 8388608 | tf_op jit(solution)/shard_map/ungate/pallas_call | solution.py:283
  91.2 0.0 collective-permute-done.2.r3_ref
  91.2 0.0 collective-permute-done.1.r2_ref
  91.2 0.0 collective-permute-done.r1_ref
  91.2 0.8 gather.1
  (2 shorter events, 0.0 us)
Async XLA Ops:
  3.3 43.0 %copy-start = (bf16[256,512]{1,0:T(8,128)(2,1)S(1)}, bf16[256,512]{1,0:T(8,128)(2,1)}, u32[]{:S(2)}) copy-start(bf16[256,512]{1,0:T(8,128)(2,1)} %constant.45.clone.last_ref) | copy-start | bytes 786436
  3.3 42.9 %copy-start.1 = (f32[2,256,128]{2,1,0:T(8,128)S(1)}, f32[2,256,128]{2,1,0:T(8,128)}, u32[]{:S(2)}) copy-start(f32[2,256,128]{2,1,0:T(8,128)} %constant.44.clone.untwist_ref) | copy-start | bytes 786436
  3.3 42.9 %copy-start.2 = (f32[2,256,128]{2,1,0:T(8,128)S(1)}, f32[2,256,128]{2,1,0:T(8,128)}, u32[]{:S(2)}) copy-start(f32[2,256,128]{2,1,0:T(8,128)} %constant.41.clone.twist_ref) | copy-start | bytes 786436
  3.3 42.9 %copy-start.3 = (bf16[512,256]{1,0:T(8,128)(2,1)S(1)}, bf16[512,256]{1,0:T(8,128)(2,1)}, u32[]{:S(2)}) copy-start(bf16[512,256]{1,0:T(8,128)(2,1)} %constant.40.clone.first_ref) | copy-start | bytes 786436
  3.3 42.9 %copy-start.4 = (bf16[256,256]{1,0:T(8,128)(2,1)S(1)}, bf16[256,256]{1,0:T(8,128)(2,1)}, u32[]{:S(2)}) copy-start(bf16[256,256]{1,0:T(8,128)(2,1)} %constant.43.clone.inverse_ref) | copy-start | bytes 393220
  3.3 42.9 %copy-start.5 = (bf16[256,256]{1,0:T(8,128)(2,1)S(1)}, bf16[256,256]{1,0:T(8,128)(2,1)}, u32[]{:S(2)}) copy-start(bf16[256,256]{1,0:T(8,128)(2,1)} %constant.42.clone.second_ref) | copy-start | bytes 393220
  53.5 34.7 %all-to-all-start.1 = ((bf16[128,8,8,128]{3,2,1,0:T(8,128)(2,1)}), bf16[128,8,8,128]{3,2,1,0:T(8,128)(2,1)S(1)}, u32[]{:S(2)}, u32[]{:S(2)}) async-start(bf16[128,8,8,128]{3,2,1,0:T(8,128)(2,1)} %bitcast.33), calls=%async_computation.1 | async-start | bytes 4194304 | tf_op jit(solution)/shard_map/all_to_all | solution.py:326
  59.7 31.6 %collective-permute-start.2 = (bf16[8,32,128]{2,1,0:T(8,128)(2,1)S(1)}, bf16[8,32,128]{2,1,0:T(8,128)(2,1)S(1)}, u32[]{:S(2)}, u32[]{:S(2)}) collective-permute-start(bf16[8,32,128]{2,1,0:T(8,128)(2,1)S(1)} %get-tuple-element.14), channel_id=1, source_target_pairs={{0,96},{32,64},{64,32},{96,0},{1,97},{33,65},{65,33},{97,1},{2,98}... | collective-permute-start | bytes 196616 | tf_op jit(solution)/shard_map/ppermute | solution.py:320
  63.3 28.0 %collective-permute-start.1 = (bf16[8,32,128]{2,1,0:T(8,128)(2,1)S(1)}, bf16[8,32,128]{2,1,0:T(8,128)(2,1)S(1)}, u32[]{:S(2)}, u32[]{:S(2)}) collective-permute-start(bf16[8,32,128]{2,1,0:T(8,128)(2,1)S(1)} %get-tuple-element.15), channel_id=1, source_target_pairs={{0,64},{32,96},{64,0},{96,32},{1,65},{33,97},{65,1},{97,33},{2,66}... | collective-permute-start | bytes 196616 | tf_op jit(solution)/shard_map/ppermute | solution.py:320
  63.7 27.6 %collective-permute-start = (bf16[8,32,128]{2,1,0:T(8,128)(2,1)S(1)}, bf16[8,32,128]{2,1,0:T(8,128)(2,1)S(1)}, u32[]{:S(2)}, u32[]{:S(2)}) collective-permute-start(bf16[8,32,128]{2,1,0:T(8,128)(2,1)S(1)} %get-tuple-element.16), channel_id=1, source_target_pairs={{0,32},{32,0},{64,96},{96,64},{1,33},{33,1},{65,97},{97,65},{2,34}... | collective-permute-start | bytes 196616 | tf_op jit(solution)/shard_map/ppermute | solution.py:320
